TPU v7x, 128 devices: a whole 4x4x4 slice. The times are simulated.
128 devices in a mesh: dp: 4 (over x), fsdp: 32 (over z, y, core).
Axes of the slice: x: 4, y: 4, z: 4, core: 2. Of those that a mesh axis runs over, the one named last changes fastest.
Arguments:
- hidden: bfloat16 [16384, 8192], P(('dp', 'fsdp')), may hold values from -6 to 6
- queries: bfloat16 [16384, 4096], P(('dp', 'fsdp')), may hold values from -170 to 170
- norm_gain: float32 [8192], replicated, may hold values from 0.1 to 1.9
- key_value_weight: bfloat16 [8192, 1024], P('fsdp'), may hold values from -0.0625 to 0.0625
- head_weight: bfloat16 [8192], replicated, may hold values from -0.0625 to 0.0625
- head_fold: bfloat16 [4096], replicated, may hold values from -0.09375 to 0.09375
- route: int32 [2, 16384], P(None, ('dp', 'fsdp')), may hold values from 0 to 127, as said below
- segments: int32 [4, 4096], P('dp'), may hold values from 0 to 7, never falling along the last dimension, each value on 1 to 2048 neighbouring positions
Outputs:
- scores: float32 [16384], P(('dp', 'fsdp'))
Inputs may be any that keep to these rules, and one draw needn't show every extreme that they name: `route`: each device sends exactly 32 tokens to each of the 4 bins, all in the block of its own fsdp index, and each bin device receives exactly 32 tokens from each of 4 devices; the bin rows of all tokens are all different and fill every bin. `segments`: documents are runs of equal numbers that never fall along a bin.
All inputs are finite; a program needn't handle non-finite values.
Results may differ from a plain program's by a relative error of at most 0.0042.
Values may be sent and summed in bfloat16 or wider, within the bound.
A program may use at most 128 MiB of HBM per device.

v0:
```python
import functools

import jax
import jax.numpy as jnp
from jax import lax
from jax.experimental import pallas as pl
from jax.experimental.pallas import tpu as pltpu
from jax.sharding import PartitionSpec as P

MESH = pl.DeviceIdType.MESH
BF = jnp.bfloat16
F32 = jnp.float32
LOG2E = 1.4426950408889634
NEG = -1e30
WROWS = 288
KROWS = 144


def nn(a, b):
    return lax.dot_general(a, b, (((1,), (0,)), ((), ())), preferred_element_type=F32)


def nt(a, b):
    return lax.dot_general(a, b, (((1,), (1,)), ((), ())), preferred_element_type=F32)


def iota(shape, axis):
    return lax.broadcasted_iota(jnp.int32, shape, axis)


def kernel(
    hid_hbm, q_hbm, gain_ref, w_hbm, hw_ref, fold_ref, route_ref, seg_ref, out_ref,
    hid, qv, wv, wpair, x3, wg, qout, qin, qx, kvout, kvin, win, kext, bias, onehot, onehot_t,
    kacc, vacc, high, acc, ret_out, ret_in,
    load_sem, pair_send, pair_recv, xs_sem, xr_sem, qs_sem, qr_sem, ks_sem, kr_sem,
    rs_sem, rr_sem, ws_sem, wr_sem, gs_sem, gr_sem,
):
    d = lax.axis_index("dp")
    f = lax.axis_index("fsdp")
    chip = f // 2
    core = f % 2
    y = chip % 4
    z = chip // 4

    def chip_at(par, u, v):
        return (1 - par) * (4 * v + u) + par * (4 * u + v)

    def coords(par):
        return (1 - par) * y + par * z, (1 - par) * z + par * y

    def near(par, du, dv):
        u, v = coords(par)
        return chip_at(par, (u + du + 4) % 4, (v + dv + 4) % 4)

    load_w = pltpu.make_async_copy(w_hbm, wv, load_sem.at[0])
    load_h = pltpu.make_async_copy(hid_hbm, hid, load_sem.at[1])
    load_q = pltpu.make_async_copy(q_hbm, qv, load_sem.at[2])
    load_w.start()
    load_h.start()
    load_q.start()

    barrier = pltpu.get_barrier_semaphore()
    peers = [(d, 2 * chip + (1 - core))]
    for dd in range(1, 4):
        for c in range(2):
            peers.append(((d + dd) % 4, 2 * chip + c))
    for du, dv in ((1, 0), (-1, 0), (0, 1), (0, -1)):
        peers.append((d, 2 * near(0, du, dv) + core))
    for peer in peers:
        pl.semaphore_signal(barrier, inc=1, device_id=peer, device_id_type=MESH)

    load_w.wait()
    fold = fold_ref[...].astype(F32)
    head_row = jnp.concatenate(
        [fold[:, h * 128 : (h + 1) * 128] for h in range(32)], axis=0
    )
    fold_t = jnp.concatenate([head_row] * 4, axis=1)
    fold_t = jnp.where(iota((32, 512), 0) // 8 == iota((32, 512), 1) // 128, fold_t, 0.0).astype(BF)
    wf = nt(fold_t, wv[:, 512:1024])
    wf_hi = wf.astype(BF).astype(F32)
    wf_lo = wf - wf_hi
    packs = []
    for c in range(2):
        rows = []
        for g in range(2):
            at = 16 * c + 8 * g
            rows += [wf_hi[at : at + 8], wf_lo[at : at + 8]]
        packs.append(jnp.concatenate(rows, axis=0).astype(BF))
    mine = pl.ds(pl.multiple_of(core * WROWS, 32), 256)
    mine_v = pl.ds(pl.multiple_of(core * WROWS + 256, 32), 32)
    own_is_1 = core == 1
    wg[chip, mine, :] = jnp.where(own_is_1, wv[:, 256:512], wv[:, 0:256])
    wg[chip, mine_v, :] = jnp.where(own_is_1, packs[1], packs[0])
    wpair[0:256, :] = jnp.where(own_is_1, wv[:, 0:256], wv[:, 256:512])
    wpair[256:288, :] = jnp.where(own_is_1, packs[0], packs[1])

    pl.semaphore_wait(barrier, len(peers))

    pair = pltpu.make_async_remote_copy(
        src_ref=wpair,
        dst_ref=wg.at[chip, pl.ds(pl.multiple_of(core * WROWS, 32), WROWS)],
        send_sem=pair_send, recv_sem=pair_recv,
        device_id=(d, 2 * chip + 1 - core), device_id_type=MESH,
    )
    pair_in = pltpu.make_async_remote_copy(
        src_ref=wpair,
        dst_ref=wg.at[chip, pl.ds(pl.multiple_of((1 - core) * WROWS, 32), WROWS)],
        send_sem=pair_send, recv_sem=pair_recv,
        device_id=(d, 2 * chip + 1 - core), device_id_type=MESH,
    )
    pair.start()

    class Gather:
        def __init__(self, buf, half, cut, send, recv):
            self.buf, self.half, self.cut = buf, half, cut
            self.sends, self.recvs = send, recv

        def part(self, par, kind):
            if kind < 2:
                off, n = 0, self.half
            elif kind == 2:
                off, n = 0, self.cut
            else:
                off, n = self.cut, self.half - self.cut
            return pl.ds(pl.multiple_of(par * self.half + off, 16), n)

        def copy(self, par, group, kind, incoming):
            step = 1 if kind in (0, 2) else -1
            hops = (1 if kind < 2 else 2) if incoming else (0 if kind < 2 else 1)
            back = -step * hops
            if group == 0:
                at = near(par, back, 0)
                to = near(par, step, 0)
            else:
                du = (0, -1, 1, 2)[group - 1]
                at = near(par, du, back)
                to = near(par, 0, step)
            ref = self.buf.at[at, self.part(par, kind)]
            return pltpu.make_async_remote_copy(
                src_ref=ref, dst_ref=ref,
                send_sem=self.sends.at[par, group, kind],
                recv_sem=self.recvs.at[par, group, kind],
                device_id=(d, 2 * to + core), device_id_type=MESH,
            )

        def send(self, par, group, kind):
            self.copy(par, group, kind, False).start()

        def wait(self, par, group, kind):
            self.copy(par, group, kind, True).wait_recv()

        def finish(self):
            for par in range(2):
                for group in range(5):
                    for kind in range(4):
                        self.copy(par, group, kind, False).wait_send()

        def begin(self, par):
            for group, kind in ((0, 0), (0, 1), (1, 0), (1, 1)):
                self.send(par, group, kind)

        def step1(self):
            for kind in range(2):
                for par in range(2):
                    self.wait(par, 0, kind)
                    self.send(par, 2 + kind, 0)
                    self.send(par, 2 + kind, 1)
                    self.send(par, 0, 2 + kind)

        def step2(self):
            for kind in range(2):
                for par in range(2):
                    self.wait(par, 1, kind)
                    self.send(par, 1, 2 + kind)

        def step3(self):
            for par in range(2):
                self.wait(par, 0, 2)
                self.wait(par, 0, 3)
                self.send(par, 4, 0)
                self.send(par, 4, 1)

        def step4(self):
            for group in (2, 3):
                for kind in range(2):
                    for par in range(2):
                        self.wait(par, group, kind)
                        self.send(par, group, 2 + kind)

        def step5(self):
            for kind in range(2):
                for par in range(2):
                    self.wait(par, 4, kind)
                    self.send(par, 4, 2 + kind)

        def step6(self, group):
            for par in range(2):
                self.wait(par, group, 2)
                self.wait(par, group, 3)

    weights = Gather(wg, WROWS, WROWS // 2, ws_sem, wr_sem)
    keys = Gather(win, KROWS, 80, gs_sem, gr_sem)

    weights.begin(core)
    pair_in.wait_recv()
    weights.begin(1 - core)

    route = route_ref[...]
    bins = jnp.broadcast_to(route[0:1, :], (128, 128))
    offs = jnp.broadcast_to(route[1:2, :], (128, 128))
    i0 = iota((128, 128), 0)
    i1 = iota((128, 128), 1)
    member = (bins == i0).astype(F32)
    before = (i0 < i1).astype(BF)
    count = nn(member.astype(BF), before)
    rank = jnp.sum(member * count, axis=0, keepdims=True)
    slot = route[0:1, :].astype(F32) * 32.0 + rank
    perm = (jnp.broadcast_to(slot, (128, 128)) == i0.astype(F32)).astype(BF)
    eye = i0 == i1
    off_col = jnp.sum(jnp.where(eye, offs.astype(F32), 0.0), axis=1, keepdims=True)
    bin_col = jnp.sum(jnp.where(eye, bins.astype(F32), 0.0), axis=1, keepdims=True)
    rank_col = jnp.sum(jnp.where(eye, jnp.broadcast_to(rank, (128, 128)), 0.0), axis=1, keepdims=True)

    load_q.wait()
    off_sorted = nn(perm, jnp.broadcast_to(off_col, (128, 128)).astype(BF)).astype(BF)
    for c in range(2):
        for b in range(4):
            qout[b, c, :, 2048:2176] = off_sorted[b * 32 : (b + 1) * 32]

    def sort_q(i, _):
        for c in range(2):
            src = pl.ds(pl.multiple_of(c * 2048 + i * 256, 256), 256)
            dst = pl.ds(pl.multiple_of(i * 256, 256), 256)
            block = nn(perm, qv[:, src]).astype(BF)
            for b in range(4):
                qout[b, c, :, dst] = block[b * 32 : (b + 1) * 32]
        return 0

    lax.fori_loop(0, 8, sort_q, 0)

    def q_copy(dd, c):
        b = (d + dd) % 4
        to = (core + c) % 2
        n = dd * 2 + c
        return pltpu.make_async_remote_copy(
            src_ref=qout.at[b, to], dst_ref=qin.at[d, core],
            send_sem=qs_sem.at[n], recv_sem=qr_sem.at[n],
            device_id=(b, 2 * chip + to), device_id_type=MESH,
        )

    def q_arrival(dd, c):
        n = dd * 2 + c
        return pltpu.make_async_remote_copy(
            src_ref=qout.at[d, core], dst_ref=qin.at[(d - dd + 4) % 4, (core + c) % 2],
            send_sem=qs_sem.at[n], recv_sem=qr_sem.at[n],
            device_id=(d, 2 * chip + 1 - core), device_id_type=MESH,
        )

    q_pairs = [(dd, c) for dd in range(4) for c in range(2) if dd or c]
    for dd, c in q_pairs:
        q_copy(dd, c).start()
    qin[d, core] = qout[d, core]

    load_h.wait()

    def squares(i, carry):
        total, dot = carry
        at = pl.ds(pl.multiple_of(i * 256, 256), 256)
        x = hid[:, at].astype(F32)
        return total + x * x, dot + x * hw_ref[:, at].astype(F32)

    zero = jnp.zeros((128, 256), F32)
    total, dot = lax.fori_loop(0, 32, squares, (zero, zero))
    root = lax.rsqrt(jnp.sum(total, axis=1, keepdims=True) * (1.0 / 8192.0) + 1e-05)
    residual = jnp.sum(dot, axis=1, keepdims=True)
    my_rows = pl.ds(pl.multiple_of(core * 128, 128), 128)

    def normalise(i, _):
        at = pl.ds(pl.multiple_of(i * 256, 256), 256)
        normed = (hid[:, at].astype(F32) * root * gain_ref[:, at]).astype(BF)
        x3[i, my_rows, :] = nn(perm, normed).astype(BF)
        return 0

    lax.fori_loop(0, 32, normalise, 0)
    x_rows = x3.at[:, my_rows, :]
    x_copy = pltpu.make_async_remote_copy(
        src_ref=x_rows, dst_ref=x_rows, send_sem=xs_sem, recv_sem=xr_sem,
        device_id=(d, 2 * chip + 1 - core), device_id_type=MESH,
    )
    other_rows = x3.at[:, pl.ds(pl.multiple_of((1 - core) * 128, 128), 128), :]
    x_in = pltpu.make_async_remote_copy(
        src_ref=other_rows, dst_ref=other_rows, send_sem=xs_sem, recv_sem=xr_sem,
        device_id=(d, 2 * chip + 1 - core), device_id_type=MESH,
    )
    x_copy.start()
    weights.step1()

    def segment_keys(i, _):
        at = pl.ds(pl.multiple_of(i * 256, 256), 256)
        s = jnp.broadcast_to(seg_ref[:, at], (128, 256))
        k = iota((128, 256), 0)
        part = jnp.where((k < 8) & (s != k), NEG, 0.0)
        kext[i] = part.T.astype(BF)
        return 0

    lax.fori_loop(0, 16, segment_keys, 0)

    x_in.wait_recv()
    kacc[...] = jnp.zeros_like(kacc)
    vacc[...] = jnp.zeros_like(vacc)

    def project(par, du, dv):
        c = near(par, du, dv)
        x = x3[2 * c + par]
        base = par * WROWS
        kacc[...] += nn(x, wg[c, pl.ds(pl.multiple_of(base, 32), 256), :])
        vacc[...] += nt(wg[c, pl.ds(pl.multiple_of(base + 256, 32), 32), :], x)

    def project_all(places):
        for du, dv in places:
            def body(par, _, du=du, dv=dv):
                project(par, du, dv)
                return 0

            lax.fori_loop(0, 2, body, 0)

    project_all([(0, 0), (-1, 0), (1, 0)])
    weights.step2()
    weights.step3()
    project_all([(0, -1), (0, 1), (2, 0)])
    weights.step4()
    project_all([(-1, -1), (-1, 1), (1, -1), (1, 1)])
    weights.step5()
    project_all([(2, -1), (2, 1)])

    for dd, c in q_pairs:
        q_arrival(dd, c).wait_recv()
    off = qin[:, :, :, 2048:2176].reshape(256, 128).astype(F32)
    arrival = iota((256, 128), 0)
    place = off + ((arrival // 32) % 2).astype(F32) * 128.0
    place = jnp.concatenate([place, place], axis=1)
    hot = (place == iota((256, 256), 1).astype(F32)).astype(F32)
    onehot[...] = hot.astype(BF)
    onehot_t[...] = hot.T.astype(BF)
    own_at = pl.ds(pl.multiple_of(chip * 256, 256), 256)
    seg_hot = (jnp.broadcast_to(seg_ref[:, own_at], (128, 256)) == iota((128, 256), 0)).astype(BF)
    qseg = nt(onehot[...], seg_hot).astype(BF)
    later = jnp.where(iota((256, 256), 0) > iota((256, 256), 1), NEG, 0.0).astype(BF)
    bias[...] = nt(later, onehot[...])
    for h in range(16):
        qx[h, :, 0:128] = qin[:, :, :, h * 128 : (h + 1) * 128].reshape(256, 128)
        qx[h, :, 128:256] = qseg

    for group, place_of in ((1, (0, 2)), (2, (-1, 2)), (3, (1, 2)), (4, (2, 2))):
        weights.step6(group)
        project_all([place_of])

    k_rows = kacc[...].astype(BF)
    v = vacc[...]
    v_rows = []
    for g in range(2):
        vf = v[g * 16 : g * 16 + 8] + v[g * 16 + 8 : g * 16 + 16]
        vf_hi = vf.astype(BF).astype(F32)
        v_rows += [vf_hi, vf - vf_hi]
    v_rows.append(jnp.zeros((96, 256), F32))
    v_cols = jnp.concatenate(v_rows, axis=0).T.astype(BF)
    for s in range(2):
        for b in range(4):
            at = s * 128 + b * 32
            kvout[b, s, :, 0:256] = k_rows[at : at + 32]
            kvout[b, s, :, 256:384] = v_cols[at : at + 32]

    def k_copy(dd):
        b = (d + dd) % 4
        return pltpu.make_async_remote_copy(
            src_ref=kvout.at[b], dst_ref=kvin.at[d],
            send_sem=ks_sem.at[dd], recv_sem=kr_sem.at[dd],
            device_id=(b, f), device_id_type=MESH,
        )

    def k_arrival(dd):
        return pltpu.make_async_remote_copy(
            src_ref=kvout.at[d], dst_ref=kvin.at[(d - dd + 4) % 4],
            send_sem=ks_sem.at[dd], recv_sem=kr_sem.at[dd],
            device_id=((d + dd) % 4, f), device_id_type=MESH,
        )

    for dd in range(1, 4):
        k_copy(dd).start()
    kvin[d] = kvout[d]
    for dd in range(1, 4):
        k_arrival(dd).wait_recv()

    got_k = kvin[:, :, :, 0:256].reshape(256, 256)
    got_v = kvin[:, :, :, 256:384].reshape(256, 128).astype(F32).T[0:32].astype(BF)
    win[chip, 0:256, :] = nn(onehot_t[...], got_k).astype(BF)
    win[chip, 256:288, :] = nn(got_v, onehot[...]).astype(BF)
    keys.begin(0)
    keys.begin(1)

    scale = LOG2E * 128.0 ** -0.5
    ones = jnp.ones((16, 256), BF)

    def attend(c, first):
        ext = kext[c]
        for g in range(2):
            key = jnp.concatenate([win[c, 0:256, g * 128 : (g + 1) * 128], ext], axis=1)
            val = jnp.concatenate([win[c, 256 + 16 * g : 272 + 16 * g, :], ones], axis=0)

            def heads(i, _, g=g, key=key, val=val):
                for j in range(2):
                    h = g * 8 + i * 2 + j
                    s = nt(key, qx[h])
                    if first:
                        s = s + bias[...]
                        new = jnp.max(s, axis=0, keepdims=True)
                        p = jnp.exp2((s - new) * scale).astype(BF)
                        acc[h] = nn(val, p)
                    else:
                        old = high[h]
                        new = jnp.maximum(old, jnp.max(s, axis=0, keepdims=True))
                        p = jnp.exp2((s - new) * scale).astype(BF)
                        acc[h] = acc[h] * jnp.exp2((old - new) * scale) + nn(val, p)
                    high[h] = new
                return 0

            lax.fori_loop(0, 4, heads, 0)

    def attend_near(dy, dz):
        c = near(0, dy, dz)

        @pl.when((c < chip) & (c >= chip - 8))
        def _():
            attend(c, False)

    attend(chip, True)
    keys.step1()
    keys.step2()
    keys.step3()
    keys.step4()
    keys.step5()
    for group in range(1, 5):
        keys.step6(group)
    for dy in range(4):
        for dz in range(4):
            if dy or dz:
                attend_near(dy, dz)

    branch = jnp.zeros((1, 256), F32)
    for h in range(16):
        a = acc[h]
        j = h % 8
        branch = branch + (a[j : j + 1] + a[8 + j : 9 + j]) / a[16:17]
    ret_out[...] = jnp.broadcast_to(branch, (8, 256))

    def r_copy(dd, c):
        n = dd * 2 + c
        return pltpu.make_async_remote_copy(
            src_ref=ret_out, dst_ref=ret_in.at[d, core],
            send_sem=rs_sem.at[n], recv_sem=rr_sem.at[n],
            device_id=((d + dd) % 4, 2 * chip + (core + c) % 2), device_id_type=MESH,
        )

    def r_arrival(dd, c):
        n = dd * 2 + c
        return pltpu.make_async_remote_copy(
            src_ref=ret_out, dst_ref=ret_in.at[(d - dd + 4) % 4, (core + c) % 2],
            send_sem=rs_sem.at[n], recv_sem=rr_sem.at[n],
            device_id=(d, 2 * chip + 1 - core), device_id_type=MESH,
        )

    for dd, c in q_pairs:
        r_copy(dd, c).start()
    ret_in[d, core] = ret_out[...]
    for dd, c in q_pairs:
        r_arrival(dd, c).wait_recv()

    lane = (d * 64 + core * 32).astype(F32) + rank_col
    lanes = iota((128, 256), 1).astype(F32)
    value = jnp.zeros((128, 256), F32)
    for b in range(4):
        row = ret_in[b, 0][0:1] + ret_in[b, 1][0:1]
        value = value + jnp.where((lanes == lane) & (bin_col == float(b)), row, 0.0)
    score = jnp.sum(value, axis=1, keepdims=True) + residual
    out_ref[...] = jnp.sum(jnp.where(eye, score, 0.0), axis=0, keepdims=True)

    pair.wait_send()
    x_copy.wait_send()
    weights.finish()
    keys.finish()
    for dd, c in q_pairs:
        q_copy(dd, c).wait_send()
        r_copy(dd, c).wait_send()
    for dd in range(1, 4):
        k_copy(dd).wait_send()


def on_device(
    hidden, queries, norm_gain, key_value_weight, head_weight, head_fold, route, segments
):
    vmem = pl.BlockSpec(memory_space=pltpu.VMEM)
    hbm = pl.BlockSpec(memory_space=pl.ANY)
    dma = pltpu.SemaphoreType.DMA
    out = pl.pallas_call(
        kernel,
        out_shape=jax.ShapeDtypeStruct((1, 128), F32),
        in_specs=[hbm, hbm, vmem, hbm, vmem, vmem, vmem, vmem],
        out_specs=vmem,
        scratch_shapes=[
            pltpu.VMEM((128, 8192), BF),
            pltpu.VMEM((128, 4096), BF),
            pltpu.VMEM((256, 1024), BF),
            pltpu.VMEM((WROWS, 256), BF),
            pltpu.VMEM((32, 256, 256), BF),
            pltpu.VMEM((16, 2 * WROWS, 256), BF),
            pltpu.VMEM((4, 2, 32, 2176), BF),
            pltpu.VMEM((4, 2, 32, 2176), BF),
            pltpu.VMEM((16, 256, 256), BF),
            pltpu.VMEM((4, 2, 32, 384), BF),
            pltpu.VMEM((4, 2, 32, 384), BF),
            pltpu.VMEM((16, 2 * KROWS, 256), BF),
            pltpu.VMEM((16, 256, 128), BF),
            pltpu.VMEM((256, 256), F32),
            pltpu.VMEM((256, 256), BF),
            pltpu.VMEM((256, 256), BF),
            pltpu.VMEM((256, 256), F32),
            pltpu.VMEM((32, 256), F32),
            pltpu.VMEM((16, 1, 256), F32),
            pltpu.VMEM((16, 32, 256), F32),
            pltpu.VMEM((8, 256), F32),
            pltpu.VMEM((4, 2, 8, 256), F32),
            dma((3,)),
            dma, dma, dma, dma,
            dma((8,)), dma((8,)),
            dma((4,)), dma((4,)),
            dma((8,)), dma((8,)),
            dma((2, 5, 4)), dma((2, 5, 4)),
            dma((2, 5, 4)), dma((2, 5, 4)),
        ],
        compiler_params=pltpu.CompilerParams(
            collective_id=0, has_side_effects=True, vmem_limit_bytes=48 * 1024 * 1024
        ),
        cost_estimate=pl.CostEstimate(
            flops=10_000_000_000, bytes_accessed=4_000_000, transcendentals=10_000_000
        ),
    )(
        hidden, queries, norm_gain.reshape(1, -1), key_value_weight,
        head_weight.reshape(1, -1), head_fold.reshape(1, -1), route, segments,
    )
    return out.reshape(-1)


def solution(mesh):
    in_specs = (
        P(("dp", "fsdp"), None),
        P(("dp", "fsdp"), None),
        P(),
        P("fsdp", None),
        P(),
        P(),
        P(None, ("dp", "fsdp")),
        P("dp", None),
    )
    out_specs = P(("dp", "fsdp"))
    return jax.shard_map(
        on_device, mesh=mesh, in_specs=in_specs, out_specs=out_specs, check_vma=False
    )
```

profile of v0, /device:TPU:65, one launch (start us, length us, event | category | flops | bytes accessed | tf_op | source)
XLA Modules:
  0.0 122.0 jit_solution(761682538931803755)
XLA Ops:
  0.0 0.7 reshape.14.fold_ref
  0.7 0.7 reshape.13.hw_ref
  1.5 0.0 copy-start
  1.5 1.6 %copy-done = bf16[128,8192]{1,0:T(8,128)(2,1)S(1)} copy-done((bf16[128,8192]{1,0:T(8,128)(2,1)S(1)}, bf16[128,8192]{1,0:T(8,128)(2,1)}, u32[]{:S(2)}) %copy-start) | copy-done | bytes 2097176
  3.0 0.0 copy-start.1
  3.0 1.2 %copy-done.1 = bf16[128,4096]{1,0:T(8,128)(2,1)S(1)} copy-done((bf16[128,4096]{1,0:T(8,128)(2,1)S(1)}, bf16[128,4096]{1,0:T(8,128)(2,1)}, u32[]{:S(2)}) %copy-start.1) | copy-done | bytes 1048600
  4.3 0.0 copy-start.2
  4.3 1.0 copy-done.2
  5.3 0.0 copy-start.3
  5.3 0.8 copy-done.3
  6.1 0.0 copy-start.4
  6.1 0.7 copy-done.4
  6.8 0.0 copy-start.5
  6.8 0.7 copy-done.5
  7.5 114.0 %shard_map.82 = f32[1,128]{1,0:T(1,128)S(1)} custom-call(bf16[128,8192]{1,0:T(8,128)(2,1)S(1)} %copy-done, bf16[128,4096]{1,0:T(8,128)(2,1)S(1)} %copy-done.1, f32[1,8192]{1,0:T(1,128)S(1)} %bitcast.2, bf16[256,1024]{1,0:T(8,128)(2,1)S(1)} %copy-done.2, bf16[1,8192]{1,0:T(2,128)(2,1)S(1)} %reshape.13.hw_ref, bf16[1,4096]{1,0:T(2,128)(2,1)S(1)} %reshape.14.fold_ref, ...), custom_call_target="tpu_custom_call" | custom-call | flops 10000000000 | bytes 4000000 | tf_op jit(solution)/shard_map/pallas_call | solution.py:504
  121.5 0.5 copy.10
Async XLA Ops:
  1.5 1.6 %copy-start = (bf16[128,8192]{1,0:T(8,128)(2,1)S(1)}, bf16[128,8192]{1,0:T(8,128)(2,1)}, u32[]{:S(2)}) copy-start(bf16[128,8192]{1,0:T(8,128)(2,1)} %hid_hbm.1) | copy-start | bytes 6291460
  3.0 1.2 %copy-start.1 = (bf16[128,4096]{1,0:T(8,128)(2,1)S(1)}, bf16[128,4096]{1,0:T(8,128)(2,1)}, u32[]{:S(2)}) copy-start(bf16[128,4096]{1,0:T(8,128)(2,1)} %q_hbm.1) | copy-start | bytes 3145732
  4.3 1.0 copy-start.2
  5.3 0.8 copy-start.3
  6.1 0.7 copy-start.4
  6.8 0.7 copy-start.5
where the time goes:
time: 122 us
  Pallas kernels  114 us (93%)
  local copies, waits for them, and re-layouts  7.96 us (7%)
    pallas_call x1, Pallas kernels, on_device(): pl.pallas_call(kernel, out_shape=jax.ShapeDtypeStruct((1, 128), F32), in_...  114 us
    unnamed x13, local copies, waits for them, and re-layouts  6.52 us

commit v1 on v0

--- a/solution.py
+++ b/solution.py
@@ -29,9 +29,9 @@
 
 
 def kernel(
-    hid_hbm, q_hbm, gain_ref, w_hbm, hw_ref, fold_ref, route_ref, seg_ref, out_ref,
-    hid, qv, wv, wpair, x3, wg, qout, qin, qx, kvout, kvin, win, kext, bias, onehot, onehot_t,
-    kacc, vacc, high, acc, ret_out, ret_in,
+    hid_hbm, q_hbm, gain_hbm, w_hbm, hw_hbm, fold_hbm, route_hbm, seg_hbm, out_ref,
+    gain_ref, hw_ref, fold_ref, route_ref, seg_ref, hw_row, hid, qv, wv, wpair, x3, wg, qout, qin, qx, kvout, kvin, win, kext, bias, onehot, onehot_t,
+    kacc, vacc, high, acc, sbuf, ret_out, ret_in,
     load_sem, pair_send, pair_recv, xs_sem, xr_sem, qs_sem, qr_sem, ks_sem, kr_sem,
     rs_sem, rr_sem, ws_sem, wr_sem, gs_sem, gr_sem,
 ):
@@ -52,12 +52,16 @@
         u, v = coords(par)
         return chip_at(par, (u + du + 4) % 4, (v + dv + 4) % 4)
 
-    load_w = pltpu.make_async_copy(w_hbm, wv, load_sem.at[0])
-    load_h = pltpu.make_async_copy(hid_hbm, hid, load_sem.at[1])
-    load_q = pltpu.make_async_copy(q_hbm, qv, load_sem.at[2])
-    load_w.start()
-    load_h.start()
-    load_q.start()
+    loads = [
+        pltpu.make_async_copy(src, dst, load_sem.at[n])
+        for n, (src, dst) in enumerate([
+            (w_hbm, wv), (fold_hbm, fold_ref), (route_hbm, route_ref), (q_hbm, qv),
+            (hid_hbm, hid), (hw_hbm, hw_ref), (gain_hbm, gain_ref), (seg_hbm, seg_ref),
+        ])
+    ]
+    load_w, load_fold, load_route, load_q, load_h, load_hw, load_gain, load_seg = loads
+    for load in loads:
+        load.start()
 
     barrier = pltpu.get_barrier_semaphore()
     peers = [(d, 2 * chip + (1 - core))]
@@ -70,7 +74,8 @@
         pl.semaphore_signal(barrier, inc=1, device_id=peer, device_id_type=MESH)
 
     load_w.wait()
-    fold = fold_ref[...].astype(F32)
+    load_fold.wait()
+    fold = fold_ref[...].reshape(1, 4096).astype(F32)
     head_row = jnp.concatenate(
         [fold[:, h * 128 : (h + 1) * 128] for h in range(32)], axis=0
     )
@@ -205,6 +210,7 @@
     pair_in.wait_recv()
     weights.begin(1 - core)
 
+    load_route.wait()
     route = route_ref[...]
     bins = jnp.broadcast_to(route[0:1, :], (128, 128))
     offs = jnp.broadcast_to(route[1:2, :], (128, 128))
@@ -262,12 +268,16 @@
     qin[d, core] = qout[d, core]
 
     load_h.wait()
+    load_hw.wait()
+    load_gain.wait()
+    load_seg.wait()
+    hw_row[...] = hw_ref[...].reshape(1, 8192).astype(F32)
 
     def squares(i, carry):
         total, dot = carry
         at = pl.ds(pl.multiple_of(i * 256, 256), 256)
         x = hid[:, at].astype(F32)
-        return total + x * x, dot + x * hw_ref[:, at].astype(F32)
+        return total + x * x, dot + x * hw_row[:, at]
 
     zero = jnp.zeros((128, 256), F32)
     total, dot = lax.fori_loop(0, 32, squares, (zero, zero))
@@ -344,12 +354,13 @@
     onehot_t[...] = hot.T.astype(BF)
     own_at = pl.ds(pl.multiple_of(chip * 256, 256), 256)
     seg_hot = (jnp.broadcast_to(seg_ref[:, own_at], (128, 256)) == iota((128, 256), 0)).astype(BF)
-    qseg = nt(onehot[...], seg_hot).astype(BF)
+    qseg = nt(seg_hot, onehot[...]).astype(BF)
     later = jnp.where(iota((256, 256), 0) > iota((256, 256), 1), NEG, 0.0).astype(BF)
     bias[...] = nt(later, onehot[...])
     for h in range(16):
-        qx[h, :, 0:128] = qin[:, :, :, h * 128 : (h + 1) * 128].reshape(256, 128)
-        qx[h, :, 128:256] = qseg
+        qh = qin[:, :, :, h * 128 : (h + 1) * 128].reshape(256, 128)
+        qx[h, 0:128, :] = qh.astype(F32).T.astype(BF)
+        qx[h, 128:256, :] = qseg
 
     for group, place_of in ((1, (0, 2)), (2, (-1, 2)), (3, (1, 2)), (4, (2, 2))):
         weights.step6(group)
@@ -402,49 +413,56 @@
     ones = jnp.ones((16, 256), BF)
 
     def attend(c, first):
-        ext = kext[c]
-        for g in range(2):
-            key = jnp.concatenate([win[c, 0:256, g * 128 : (g + 1) * 128], ext], axis=1)
-            val = jnp.concatenate([win[c, 256 + 16 * g : 272 + 16 * g, :], ones], axis=0)
-
-            def heads(i, _, g=g, key=key, val=val):
-                for j in range(2):
-                    h = g * 8 + i * 2 + j
-                    s = nt(key, qx[h])
-                    if first:
-                        s = s + bias[...]
-                        new = jnp.max(s, axis=0, keepdims=True)
-                        p = jnp.exp2((s - new) * scale).astype(BF)
-                        acc[h] = nn(val, p)
-                    else:
-                        old = high[h]
-                        new = jnp.maximum(old, jnp.max(s, axis=0, keepdims=True))
-                        p = jnp.exp2((s - new) * scale).astype(BF)
-                        acc[h] = acc[h] * jnp.exp2((old - new) * scale) + nn(val, p)
-                    high[h] = new
-                return 0
-
-            lax.fori_loop(0, 4, heads, 0)
-
-    def attend_near(dy, dz):
-        c = near(0, dy, dz)
-
-        @pl.when((c < chip) & (c >= chip - 8))
-        def _():
-            attend(c, False)
+        def scores(h):
+            g = h // 8
+            key = jnp.concatenate([win[c, 0:256, g * 128 : (g + 1) * 128], kext[c]], axis=1)
+            s = nn(key, qx[h])
+            sbuf[h % 8] = s + bias[...] if first else s
+
+        for h in range(4):
+            scores(h)
+        for batch in range(0, 16, 4):
+            for h in range(batch + 4, min(batch + 8, 16)):
+                scores(h)
+            for h in range(batch, batch + 4):
+                g = h // 8
+                val = jnp.concatenate([win[c, 256 + 16 * g : 272 + 16 * g, :], ones], axis=0)
+                s = sbuf[h % 8]
+                new = jnp.max(s, axis=0, keepdims=True)
+                if not first:
+                    old = high[h]
+                    new = jnp.maximum(old, new)
+                p = jnp.exp2((s - new) * scale).astype(BF)
+                part = nn(val, p)
+                acc[h] = part if first else acc[h] * jnp.exp2((old - new) * scale) + part
+                high[h] = new
+
+    def attend_list(count, place):
+        def body(i, _):
+            dy, dz = place(i)
+            c = near(0, dy, dz)
+
+            @pl.when((c < chip) & (c >= chip - 8))
+            def _():
+                attend(c, False)
+
+            return 0
+
+        lax.fori_loop(0, count, body, 0)
 
     attend(chip, True)
     keys.step1()
     keys.step2()
     keys.step3()
+    attend_list(4, lambda i: ((1 - 2 * (i % 2)) * (1 - i // 2), (1 - 2 * (i % 2)) * (i // 2)))
     keys.step4()
     keys.step5()
+    attend_list(4, lambda i: (1 - 2 * (i % 2), 1 - 2 * (i // 2)))
     for group in range(1, 5):
         keys.step6(group)
-    for dy in range(4):
-        for dz in range(4):
-            if dy or dz:
-                attend_near(dy, dz)
+    attend_list(7, lambda i: (
+        2 * (1 - i // 4) + (i - 5) * (i // 4), (i - 1) * (1 - i // 4) + 2 * (i // 4)
+    ))
 
     branch = jnp.zeros((1, 256), F32)
     for h in range(16):
@@ -504,9 +522,15 @@
     out = pl.pallas_call(
         kernel,
         out_shape=jax.ShapeDtypeStruct((1, 128), F32),
-        in_specs=[hbm, hbm, vmem, hbm, vmem, vmem, vmem, vmem],
+        in_specs=[hbm] * 8,
         out_specs=vmem,
         scratch_shapes=[
+            pltpu.VMEM((1, 8192), F32),
+            pltpu.VMEM((8192,), BF),
+            pltpu.VMEM((4096,), BF),
+            pltpu.VMEM((2, 128), jnp.int32),
+            pltpu.VMEM((1, 4096), jnp.int32),
+            pltpu.VMEM((1, 8192), F32),
             pltpu.VMEM((128, 8192), BF),
             pltpu.VMEM((128, 4096), BF),
             pltpu.VMEM((256, 1024), BF),
@@ -527,9 +551,10 @@
             pltpu.VMEM((32, 256), F32),
             pltpu.VMEM((16, 1, 256), F32),
             pltpu.VMEM((16, 32, 256), F32),
+            pltpu.VMEM((8, 256, 256), F32),
             pltpu.VMEM((8, 256), F32),
             pltpu.VMEM((4, 2, 8, 256), F32),
-            dma((3,)),
+            dma((8,)),
             dma, dma, dma, dma,
             dma((8,)), dma((8,)),
             dma((4,)), dma((4,)),
@@ -538,14 +563,14 @@
             dma((2, 5, 4)), dma((2, 5, 4)),
         ],
         compiler_params=pltpu.CompilerParams(
-            collective_id=0, has_side_effects=True, vmem_limit_bytes=48 * 1024 * 1024
+            collective_id=0, has_side_effects=True, vmem_limit_bytes=62 * 1024 * 1024
         ),
         cost_estimate=pl.CostEstimate(
             flops=10_000_000_000, bytes_accessed=4_000_000, transcendentals=10_000_000
         ),
     )(
         hidden, queries, norm_gain.reshape(1, -1), key_value_weight,
-        head_weight.reshape(1, -1), head_fold.reshape(1, -1), route, segments,
+        head_weight, head_fold, route, segments,
     )
     return out.reshape(-1)
 

time: 122 us -> 74.2 us (0.61)
  Pallas kernels: 114 us -> 72.8 us
  local copies, waits for them, and re-layouts: 7.96 us -> 1.19 us
    pallas_call x1, Pallas kernels: 114 us -> 72.8 us  [on_device(): pl.pallas_call(kernel, out_shape=jax.ShapeDtypeStruct((1, 128), F32), in_...]
    unnamed x13 -> x1, local copies, waits for them, and re-layouts: 6.52 us -> 1.19 us
    reshape x2 -> x0, local copies, waits for them, and re-layouts: 1.45 us -> none  [the longest x1 0.74 us: on_device(): head_weight.reshape(1, -1)]
where the time goes in v1:
time: 74.2 us; the launch traced here: 74 us
  Pallas kernels  72.8 us (98%)
  local copies, waits for them, and re-layouts  1.19 us (2%)
    pallas_call x1, Pallas kernels, on_device(): pl.pallas_call(kernel, out_shape=jax.ShapeDtypeStruct((1, 128), F32), in_...  72.8 us

profile of v1, /device:TPU:65, one launch (start us, length us, event | category | flops | bytes accessed | tf_op | source)
XLA Modules:
  0.0 74.0 jit_solution(18288855900416975268)
XLA Ops:
  0.0 72.8 %shard_map.82 = f32[1,128]{1,0:T(1,128)} custom-call(bf16[128,8192]{1,0:T(8,128)(2,1)} %hid_hbm.1, bf16[128,4096]{1,0:T(8,128)(2,1)} %q_hbm.1, f32[1,8192]{1,0:T(1,128)} %bitcast.2, bf16[256,1024]{1,0:T(8,128)(2,1)} %w_hbm.1, bf16[8192]{0:T(1024)(128)(2,1)} %hw_hbm.1, bf16[4096]{0:T(1024)(128)(2,1)} %fold_hbm.1, s32[2,128]{1,0:T(2,128)} %route_hbm.1, ...), custom_call_target="tpu_custom_call" | custom-call | flops 10000000000 | bytes 4000000 | tf_op jit(solution)/shard_map/pallas_call | solution.py:522
  72.8 1.2 %copy.10 = f32[128]{0:T(128)} copy(f32[128]{0:T(128)} %bitcast.3) | data formatting | bytes 1024

commit v2 on v1

--- a/solution.py
+++ b/solution.py
@@ -52,6 +52,16 @@
         u, v = coords(par)
         return chip_at(par, (u + du + 4) % 4, (v + dv + 4) % 4)
 
+    barrier = pltpu.get_barrier_semaphore()
+    peers = [(d, 2 * chip + (1 - core))]
+    for dd in range(1, 4):
+        for c in range(2):
+            peers.append(((d + dd) % 4, 2 * chip + c))
+    for du, dv in ((1, 0), (-1, 0), (0, 1), (0, -1), (2, 0), (0, 2)):
+        peers.append((d, 2 * near(0, du, dv) + core))
+    for peer in peers:
+        pl.semaphore_signal(barrier, inc=1, device_id=peer, device_id_type=MESH)
+
     loads = [
         pltpu.make_async_copy(src, dst, load_sem.at[n])
         for n, (src, dst) in enumerate([
@@ -62,16 +72,6 @@
     load_w, load_fold, load_route, load_q, load_h, load_hw, load_gain, load_seg = loads
     for load in loads:
         load.start()
-
-    barrier = pltpu.get_barrier_semaphore()
-    peers = [(d, 2 * chip + (1 - core))]
-    for dd in range(1, 4):
-        for c in range(2):
-            peers.append(((d + dd) % 4, 2 * chip + c))
-    for du, dv in ((1, 0), (-1, 0), (0, 1), (0, -1)):
-        peers.append((d, 2 * near(0, du, dv) + core))
-    for peer in peers:
-        pl.semaphore_signal(barrier, inc=1, device_id=peer, device_id_type=MESH)
 
     load_w.wait()
     load_fold.wait()
@@ -84,41 +84,44 @@
     wf = nt(fold_t, wv[:, 512:1024])
     wf_hi = wf.astype(BF).astype(F32)
     wf_lo = wf - wf_hi
-    packs = []
-    for c in range(2):
-        rows = []
-        for g in range(2):
+    own_is_1 = core == 1
+    for g in range(2):
+        packs = []
+        for c in range(2):
             at = 16 * c + 8 * g
-            rows += [wf_hi[at : at + 8], wf_lo[at : at + 8]]
-        packs.append(jnp.concatenate(rows, axis=0).astype(BF))
-    mine = pl.ds(pl.multiple_of(core * WROWS, 32), 256)
-    mine_v = pl.ds(pl.multiple_of(core * WROWS + 256, 32), 32)
-    own_is_1 = core == 1
-    wg[chip, mine, :] = jnp.where(own_is_1, wv[:, 256:512], wv[:, 0:256])
-    wg[chip, mine_v, :] = jnp.where(own_is_1, packs[1], packs[0])
-    wpair[0:256, :] = jnp.where(own_is_1, wv[:, 0:256], wv[:, 256:512])
-    wpair[256:288, :] = jnp.where(own_is_1, packs[0], packs[1])
+            rows = [wf_hi[at : at + 8], wf_lo[at : at + 8]]
+            pack = jnp.concatenate(rows, axis=0).astype(BF)
+            packs.append((wv[:, (2 * c + g) * 128 : (2 * c + g + 1) * 128], pack))
+        base = pl.multiple_of(core * WROWS, 32)
+        for n in range(2):
+            mine = jnp.where(own_is_1, packs[1][n], packs[0][n])
+            theirs = jnp.where(own_is_1, packs[0][n], packs[1][n])
+            if n == 0:
+                wg[g, chip, pl.ds(base, 256), :] = mine
+                wpair[g, 0:256, :] = theirs
+            else:
+                for side in range(2):
+                    lanes_of = slice(side * 128, (side + 1) * 128)
+                    at = 256 + 16 * side
+                    wg[g, chip, pl.ds(base + at, 16), :] = mine[:, lanes_of]
+                    wpair[g, at : at + 16, :] = theirs[:, lanes_of]
 
     pl.semaphore_wait(barrier, len(peers))
 
-    pair = pltpu.make_async_remote_copy(
-        src_ref=wpair,
-        dst_ref=wg.at[chip, pl.ds(pl.multiple_of(core * WROWS, 32), WROWS)],
-        send_sem=pair_send, recv_sem=pair_recv,
-        device_id=(d, 2 * chip + 1 - core), device_id_type=MESH,
-    )
-    pair_in = pltpu.make_async_remote_copy(
-        src_ref=wpair,
-        dst_ref=wg.at[chip, pl.ds(pl.multiple_of((1 - core) * WROWS, 32), WROWS)],
-        send_sem=pair_send, recv_sem=pair_recv,
-        device_id=(d, 2 * chip + 1 - core), device_id_type=MESH,
-    )
-    pair.start()
+    def pair(g, side):
+        at = pl.ds(pl.multiple_of(side * WROWS, 32), WROWS)
+        return pltpu.make_async_remote_copy(
+            src_ref=wpair.at[g], dst_ref=wg.at[g, chip, at],
+            send_sem=pair_send.at[g], recv_sem=pair_recv.at[g],
+            device_id=(d, 2 * chip + 1 - core), device_id_type=MESH,
+        )
+
+    for g in range(2):
+        pair(g, core).start()
 
     class Gather:
-        def __init__(self, buf, half, cut, send, recv):
-            self.buf, self.half, self.cut = buf, half, cut
-            self.sends, self.recvs = send, recv
+        def __init__(self, g):
+            self.g, self.half, self.cut = g, WROWS, WROWS // 2
 
         def part(self, par, kind):
             if kind < 2:
@@ -140,11 +143,11 @@
                 du = (0, -1, 1, 2)[group - 1]
                 at = near(par, du, back)
                 to = near(par, 0, step)
-            ref = self.buf.at[at, self.part(par, kind)]
+            ref = wg.at[self.g, at, self.part(par, kind)]
             return pltpu.make_async_remote_copy(
                 src_ref=ref, dst_ref=ref,
-                send_sem=self.sends.at[par, group, kind],
-                recv_sem=self.recvs.at[par, group, kind],
+                send_sem=ws_sem.at[self.g, par, group, kind],
+                recv_sem=wr_sem.at[self.g, par, group, kind],
                 device_id=(d, 2 * to + core), device_id_type=MESH,
             )
 
@@ -160,9 +163,9 @@
                     for kind in range(4):
                         self.copy(par, group, kind, False).wait_send()
 
-        def begin(self, par):
-            for group, kind in ((0, 0), (0, 1), (1, 0), (1, 1)):
-                self.send(par, group, kind)
+        def begin(self, par, group):
+            self.send(par, group, 0)
+            self.send(par, group, 1)
 
         def step1(self):
             for kind in range(2):
@@ -203,12 +206,110 @@
                 self.wait(par, group, 2)
                 self.wait(par, group, 3)
 
-    weights = Gather(wg, WROWS, WROWS // 2, ws_sem, wr_sem)
-    keys = Gather(win, KROWS, 80, gs_sem, gr_sem)
-
-    weights.begin(core)
-    pair_in.wait_recv()
-    weights.begin(1 - core)
+    class Keys:
+        def __init__(self, g):
+            self.g = g
+
+        def copy(self, n, at, par, to):
+            ref = win.at[self.g, at, pl.ds(par * KROWS, KROWS)]
+            return pltpu.make_async_remote_copy(
+                src_ref=ref, dst_ref=ref,
+                send_sem=gs_sem.at[self.g, n], recv_sem=gr_sem.at[self.g, n],
+                device_id=(d, 2 * to + core), device_id_type=MESH,
+            )
+
+        def first_y(self, e, incoming):
+            at = near(0, -e if incoming else 0, 0)
+            return self.copy(e - 1, at, 0, near(0, e, 0)), True
+
+        def first_z(self, j, incoming):
+            at = near(0, 0, -j if incoming else 0)
+            return self.copy(2 + j, at, 1, near(0, 0, j)), (z >= j if incoming else z < 4 - j)
+
+        def then_z(self, k, j, incoming):
+            at = near(0, k, -j if incoming else 0)
+            ok = z >= j if incoming else z < 4 - j
+            if j == 2:
+                ok = ok & ((y + k) % 4 >= y)
+            return self.copy(5 + 2 * k + j - 1, at, 0, near(0, 0, j)), ok
+
+        def then_y(self, e, j, incoming):
+            at = near(0, -e if incoming else 0, -j)
+            source = (y - e + 4) % 4 if incoming else y
+            target = y if incoming else (y + e) % 4
+            ok = z >= j
+            if j == 0:
+                ok = source < target
+            if j == 2:
+                ok = ok & (source >= target)
+            return self.copy(13 + 3 * j + e - 1, at, 1, near(0, e, 0)), ok
+
+        def run(self, act, made):
+            copy, ok = made
+            if ok is True:
+                act(copy)
+            else:
+                @pl.when(ok)
+                def _():
+                    act(copy)
+
+        def send(self, kind, *which):
+            self.run(lambda copy: copy.start(), kind(*which, False))
+
+        def wait(self, kind, *which):
+            self.run(lambda copy: copy.wait_recv(), kind(*which, True))
+
+        def begin(self):
+            for e in (1, 3, 2):
+                self.send(self.first_y, e)
+            for j in (1, 2):
+                self.send(self.first_z, j)
+            for j in (1, 2):
+                self.send(self.then_z, 0, j)
+            for e in (1, 3, 2):
+                self.send(self.then_y, e, 0)
+
+        def forward(self):
+            self.wait(self.first_z, 1)
+            for e in (1, 3, 2):
+                self.send(self.then_y, e, 1)
+            for e in (1, 3, 2):
+                self.wait(self.first_y, e)
+                for j in (1, 2):
+                    self.send(self.then_z, (4 - e) % 4, j)
+            self.wait(self.first_z, 2)
+            for e in (1, 3, 2):
+                self.send(self.then_y, e, 2)
+
+        def row(self, j):
+            for e in (1, 3, 2):
+                self.wait(self.then_y, e, j)
+            if j:
+                for k in range(4):
+                    self.wait(self.then_z, k, j)
+
+        def finish(self):
+            done = lambda copy: copy.wait_send()
+            for e in (1, 2, 3):
+                self.run(done, self.first_y(e, False))
+                for j in range(3):
+                    self.run(done, self.then_y(e, j, False))
+            for j in (1, 2):
+                self.run(done, self.first_z(j, False))
+                for k in range(4):
+                    self.run(done, self.then_z(k, j, False))
+
+    weights = [Gather(0), Gather(1)]
+    keys = [Keys(0), Keys(1)]
+
+    for g in range(2):
+        for group in range(2):
+            if g == 0 or group == 0:
+                weights[g].begin(core, group)
+        pair(g, 1 - core).wait_recv()
+        for group in range(2):
+            if g == 0 or group == 0:
+                weights[g].begin(1 - core, group)
 
     load_route.wait()
     route = route_ref[...]
@@ -267,6 +368,10 @@
         q_copy(dd, c).start()
     qin[d, core] = qout[d, core]
 
+    weights[0].step1()
+    for par in range(2):
+        weights[1].begin(par, 1)
+
     load_h.wait()
     load_hw.wait()
     load_gain.wait()
@@ -303,7 +408,10 @@
         device_id=(d, 2 * chip + 1 - core), device_id_type=MESH,
     )
     x_copy.start()
-    weights.step1()
+    weights[0].step2()
+    weights[1].step1()
+    weights[0].step3()
+    weights[0].step4()
 
     def segment_keys(i, _):
         at = pl.ds(pl.multiple_of(i * 256, 256), 256)
@@ -319,29 +427,80 @@
     kacc[...] = jnp.zeros_like(kacc)
     vacc[...] = jnp.zeros_like(vacc)
 
-    def project(par, du, dv):
+    def project(g, par, du, dv):
         c = near(par, du, dv)
         x = x3[2 * c + par]
-        base = par * WROWS
-        kacc[...] += nn(x, wg[c, pl.ds(pl.multiple_of(base, 32), 256), :])
-        vacc[...] += nt(wg[c, pl.ds(pl.multiple_of(base + 256, 32), 32), :], x)
-
-    def project_all(places):
+        base = pl.multiple_of(par * WROWS, 32)
+        kacc[g] += nn(x, wg[g, c, pl.ds(base, 256), :])
+        vacc[g] += nt(wg[g, c, pl.ds(base + 256, 16), :], x[:, 0:128]) + nt(
+            wg[g, c, pl.ds(base + 272, 16), :], x[:, 128:256]
+        )
+
+    def project_all(g, places):
         for du, dv in places:
             def body(par, _, du=du, dv=dv):
-                project(par, du, dv)
+                project(g, par, du, dv)
                 return 0
 
             lax.fori_loop(0, 2, body, 0)
 
-    project_all([(0, 0), (-1, 0), (1, 0)])
-    weights.step2()
-    weights.step3()
-    project_all([(0, -1), (0, 1), (2, 0)])
-    weights.step4()
-    project_all([(-1, -1), (-1, 1), (1, -1), (1, 1)])
-    weights.step5()
-    project_all([(2, -1), (2, 1)])
+    def project_rest(g):
+        for group, place_of in ((1, (0, 2)), (2, (-1, 2)), (3, (1, 2)), (4, (2, 2))):
+            weights[g].step6(group)
+            project_all(g, [place_of])
+
+    def send_keys(g):
+        k_rows = kacc[g].astype(BF)
+        v = vacc[g]
+        vf = v[0:8] + v[8:16]
+        vf_hi = vf.astype(BF).astype(F32)
+        v_rows = jnp.concatenate([vf_hi, vf - vf_hi, jnp.zeros((112, 256), F32)], axis=0)
+        v_cols = v_rows.T.astype(BF)
+        for s in range(2):
+            for b in range(4):
+                at = s * 128 + b * 32
+                kvout[g, b, s, :, 0:128] = k_rows[at : at + 32]
+                kvout[g, b, s, :, 128:256] = v_cols[at : at + 32]
+        for dd in range(1, 4):
+            k_copy(g, dd).start()
+        kvin[g, d] = kvout[g, d]
+
+    def take_keys(g):
+        for dd in range(1, 4):
+            k_arrival(g, dd).wait_recv()
+        got_k = kvin[g, :, :, :, 0:128].reshape(256, 128)
+        got_v = kvin[g, :, :, :, 128:256].reshape(256, 128).astype(F32).T[0:16].astype(BF)
+        values = nn(got_v, onehot[...]).astype(BF)
+        win[g, chip, 0:256, :] = nn(onehot_t[...], got_k).astype(BF)
+        win[g, chip, 256:272, :] = values[:, 0:128]
+        win[g, chip, 272:288, :] = values[:, 128:256]
+        keys[g].begin()
+
+    def k_copy(g, dd):
+        b = (d + dd) % 4
+        return pltpu.make_async_remote_copy(
+            src_ref=kvout.at[g, b], dst_ref=kvin.at[g, d],
+            send_sem=ks_sem.at[g, dd], recv_sem=kr_sem.at[g, dd],
+            device_id=(b, f), device_id_type=MESH,
+        )
+
+    def k_arrival(g, dd):
+        return pltpu.make_async_remote_copy(
+            src_ref=kvout.at[g, d], dst_ref=kvin.at[g, (d - dd + 4) % 4],
+            send_sem=ks_sem.at[g, dd], recv_sem=kr_sem.at[g, dd],
+            device_id=((d + dd) % 4, f), device_id_type=MESH,
+        )
+
+    project_all(0, [(0, 0), (-1, 0), (1, 0), (0, -1), (0, 1), (2, 0)])
+    weights[1].step2()
+    weights[0].step5()
+    weights[1].step3()
+    project_all(0, [(-1, -1), (-1, 1), (1, -1), (1, 1), (2, -1), (2, 1)])
+    weights[1].step4()
+    project_rest(0)
+    send_keys(0)
+    weights[1].step5()
+    project_all(1, [(0, 0), (-1, 0), (1, 0), (0, -1), (0, 1), (2, 0)])
 
     for dd, c in q_pairs:
         q_arrival(dd, c).wait_recv()
@@ -352,6 +511,7 @@
     hot = (place == iota((256, 256), 1).astype(F32)).astype(F32)
     onehot[...] = hot.astype(BF)
     onehot_t[...] = hot.T.astype(BF)
+    take_keys(0)
     own_at = pl.ds(pl.multiple_of(chip * 256, 256), 256)
     seg_hot = (jnp.broadcast_to(seg_ref[:, own_at], (128, 256)) == iota((128, 256), 0)).astype(BF)
     qseg = nt(seg_hot, onehot[...]).astype(BF)
@@ -362,72 +522,27 @@
         qx[h, 0:128, :] = qh.astype(F32).T.astype(BF)
         qx[h, 128:256, :] = qseg
 
-    for group, place_of in ((1, (0, 2)), (2, (-1, 2)), (3, (1, 2)), (4, (2, 2))):
-        weights.step6(group)
-        project_all([place_of])
-
-    k_rows = kacc[...].astype(BF)
-    v = vacc[...]
-    v_rows = []
-    for g in range(2):
-        vf = v[g * 16 : g * 16 + 8] + v[g * 16 + 8 : g * 16 + 16]
-        vf_hi = vf.astype(BF).astype(F32)
-        v_rows += [vf_hi, vf - vf_hi]
-    v_rows.append(jnp.zeros((96, 256), F32))
-    v_cols = jnp.concatenate(v_rows, axis=0).T.astype(BF)
-    for s in range(2):
-        for b in range(4):
-            at = s * 128 + b * 32
-            kvout[b, s, :, 0:256] = k_rows[at : at + 32]
-            kvout[b, s, :, 256:384] = v_cols[at : at + 32]
-
-    def k_copy(dd):
-        b = (d + dd) % 4
-        return pltpu.make_async_remote_copy(
-            src_ref=kvout.at[b], dst_ref=kvin.at[d],
-            send_sem=ks_sem.at[dd], recv_sem=kr_sem.at[dd],
-            device_id=(b, f), device_id_type=MESH,
-        )
-
-    def k_arrival(dd):
-        return pltpu.make_async_remote_copy(
-            src_ref=kvout.at[d], dst_ref=kvin.at[(d - dd + 4) % 4],
-            send_sem=ks_sem.at[dd], recv_sem=kr_sem.at[dd],
-            device_id=((d + dd) % 4, f), device_id_type=MESH,
-        )
-
-    for dd in range(1, 4):
-        k_copy(dd).start()
-    kvin[d] = kvout[d]
-    for dd in range(1, 4):
-        k_arrival(dd).wait_recv()
-
-    got_k = kvin[:, :, :, 0:256].reshape(256, 256)
-    got_v = kvin[:, :, :, 256:384].reshape(256, 128).astype(F32).T[0:32].astype(BF)
-    win[chip, 0:256, :] = nn(onehot_t[...], got_k).astype(BF)
-    win[chip, 256:288, :] = nn(got_v, onehot[...]).astype(BF)
-    keys.begin(0)
-    keys.begin(1)
-
+    project_all(1, [(-1, -1), (-1, 1), (1, -1), (1, 1), (2, -1), (2, 1)])
     scale = LOG2E * 128.0 ** -0.5
     ones = jnp.ones((16, 256), BF)
 
-    def attend(c, first):
-        def scores(h):
-            g = h // 8
-            key = jnp.concatenate([win[c, 0:256, g * 128 : (g + 1) * 128], kext[c]], axis=1)
-            s = nn(key, qx[h])
-            sbuf[h % 8] = s + bias[...] if first else s
-
-        for h in range(4):
-            scores(h)
-        for batch in range(0, 16, 4):
-            for h in range(batch + 4, min(batch + 8, 16)):
-                scores(h)
-            for h in range(batch, batch + 4):
-                g = h // 8
-                val = jnp.concatenate([win[c, 256 + 16 * g : 272 + 16 * g, :], ones], axis=0)
-                s = sbuf[h % 8]
+    def attend(g, c, first):
+        def scores(j):
+            key = jnp.concatenate([win[g, c, 0:256, :], kext[c]], axis=1)
+            s = nn(key, qx[g * 8 + j])
+            sbuf[j] = s + bias[...] if first else s
+
+        for j in range(4):
+            scores(j)
+        for batch in (0, 4):
+            if batch == 0:
+                for j in range(4, 8):
+                    scores(j)
+            for j in range(batch, batch + 4):
+                h = g * 8 + j
+                values = jnp.concatenate([win[g, c, 256:272, :], win[g, c, 272:288, :]], axis=1)
+                val = jnp.concatenate([values, ones], axis=0)
+                s = sbuf[j]
                 new = jnp.max(s, axis=0, keepdims=True)
                 if not first:
                     old = high[h]
@@ -437,32 +552,34 @@
                 acc[h] = part if first else acc[h] * jnp.exp2((old - new) * scale) + part
                 high[h] = new
 
-    def attend_list(count, place):
-        def body(i, _):
-            dy, dz = place(i)
-            c = near(0, dy, dz)
-
-            @pl.when((c < chip) & (c >= chip - 8))
+    def attend_row(g, row):
+        keys[g].row(row)
+
+        def body(k, _):
+            source = (y + k) % 4
+            c = chip - y - 4 * row + source
+            seen = (z >= row) & (c < chip) & (c >= chip - 8)
+
+            @pl.when(seen)
             def _():
-                attend(c, False)
+                attend(g, c, False)
 
             return 0
 
-        lax.fori_loop(0, count, body, 0)
-
-    attend(chip, True)
-    keys.step1()
-    keys.step2()
-    keys.step3()
-    attend_list(4, lambda i: ((1 - 2 * (i % 2)) * (1 - i // 2), (1 - 2 * (i % 2)) * (i // 2)))
-    keys.step4()
-    keys.step5()
-    attend_list(4, lambda i: (1 - 2 * (i % 2), 1 - 2 * (i // 2)))
-    for group in range(1, 5):
-        keys.step6(group)
-    attend_list(7, lambda i: (
-        2 * (1 - i // 4) + (i - 5) * (i // 4), (i - 1) * (1 - i // 4) + 2 * (i // 4)
-    ))
+        lax.fori_loop(0, 4, body, 0)
+
+    project_rest(1)
+    send_keys(1)
+    keys[0].forward()
+    attend(0, chip, True)
+    take_keys(1)
+    attend_row(0, 0)
+    keys[1].forward()
+    attend_row(0, 1)
+    attend_row(0, 2)
+    attend(1, chip, True)
+    for row in range(3):
+        attend_row(1, row)
 
     branch = jnp.zeros((1, 256), F32)
     for h in range(16):
@@ -502,15 +619,17 @@
     score = jnp.sum(value, axis=1, keepdims=True) + residual
     out_ref[...] = jnp.sum(jnp.where(eye, score, 0.0), axis=0, keepdims=True)
 
-    pair.wait_send()
     x_copy.wait_send()
-    weights.finish()
-    keys.finish()
+    for g in range(2):
+        pair(g, core).wait_send()
+        weights[g].finish()
+        keys[g].finish()
     for dd, c in q_pairs:
         q_copy(dd, c).wait_send()
         r_copy(dd, c).wait_send()
-    for dd in range(1, 4):
-        k_copy(dd).wait_send()
+    for g in range(2):
+        for dd in range(1, 4):
+            k_copy(g, dd).wait_send()
 
 
 def on_device(
@@ -534,33 +653,33 @@
             pltpu.VMEM((128, 8192), BF),
             pltpu.VMEM((128, 4096), BF),
             pltpu.VMEM((256, 1024), BF),
-            pltpu.VMEM((WROWS, 256), BF),
+            pltpu.VMEM((2, WROWS, 128), BF),
             pltpu.VMEM((32, 256, 256), BF),
-            pltpu.VMEM((16, 2 * WROWS, 256), BF),
+            pltpu.VMEM((2, 16, 2 * WROWS, 128), BF),
             pltpu.VMEM((4, 2, 32, 2176), BF),
             pltpu.VMEM((4, 2, 32, 2176), BF),
             pltpu.VMEM((16, 256, 256), BF),
-            pltpu.VMEM((4, 2, 32, 384), BF),
-            pltpu.VMEM((4, 2, 32, 384), BF),
-            pltpu.VMEM((16, 2 * KROWS, 256), BF),
+            pltpu.VMEM((2, 4, 2, 32, 256), BF),
+            pltpu.VMEM((2, 4, 2, 32, 256), BF),
+            pltpu.VMEM((2, 16, 2 * KROWS, 128), BF),
             pltpu.VMEM((16, 256, 128), BF),
             pltpu.VMEM((256, 256), F32),
             pltpu.VMEM((256, 256), BF),
             pltpu.VMEM((256, 256), BF),
-            pltpu.VMEM((256, 256), F32),
-            pltpu.VMEM((32, 256), F32),
+            pltpu.VMEM((2, 256, 128), F32),
+            pltpu.VMEM((2, 16, 256), F32),
             pltpu.VMEM((16, 1, 256), F32),
             pltpu.VMEM((16, 32, 256), F32),
             pltpu.VMEM((8, 256, 256), F32),
             pltpu.VMEM((8, 256), F32),
             pltpu.VMEM((4, 2, 8, 256), F32),
             dma((8,)),
-            dma, dma, dma, dma,
+            dma((2,)), dma((2,)), dma, dma,
             dma((8,)), dma((8,)),
-            dma((4,)), dma((4,)),
+            dma((2, 4)), dma((2, 4)),
             dma((8,)), dma((8,)),
-            dma((2, 5, 4)), dma((2, 5, 4)),
-            dma((2, 5, 4)), dma((2, 5, 4)),
+            dma((2, 2, 5, 4)), dma((2, 2, 5, 4)),
+            dma((2, 22)), dma((2, 22)),
         ],
         compiler_params=pltpu.CompilerParams(
             collective_id=0, has_side_effects=True, vmem_limit_bytes=62 * 1024 * 1024

time: 74.2 us -> 71.6 us (0.965)
  Pallas kernels: 72.8 us -> 70.3 us
    pallas_call x1, Pallas kernels: 72.8 us -> 70.3 us  [on_device(): pl.pallas_call(kernel, out_shape=jax.ShapeDtypeStruct((1, 128), F32), in_...]
where the time goes in v2:
time: 71.6 us; the launch traced here: 71.5 us
  Pallas kernels  70.3 us (98%)
  local copies, waits for them, and re-layouts  1.19 us (2%)
    pallas_call x1, Pallas kernels, on_device(): pl.pallas_call(kernel, out_shape=jax.ShapeDtypeStruct((1, 128), F32), in_...  70.3 us

profile of v2, /device:TPU:65, one launch (start us, length us, event | category | flops | bytes accessed | tf_op | source)
XLA Modules:
  0.0 71.5 jit_solution(17008007149273509384)
XLA Ops:
  0.0 70.3 %shard_map.82 = f32[1,128]{1,0:T(1,128)} custom-call(bf16[128,8192]{1,0:T(8,128)(2,1)} %hid_hbm.1, bf16[128,4096]{1,0:T(8,128)(2,1)} %q_hbm.1, f32[1,8192]{1,0:T(1,128)} %bitcast.2, bf16[256,1024]{1,0:T(8,128)(2,1)} %w_hbm.1, bf16[8192]{0:T(1024)(128)(2,1)} %hw_hbm.1, bf16[4096]{0:T(1024)(128)(2,1)} %fold_hbm.1, s32[2,128]{1,0:T(2,128)} %route_hbm.1, ...), custom_call_target="tpu_custom_call" | custom-call | flops 10000000000 | bytes 4000000 | tf_op jit(solution)/shard_map/pallas_call | solution.py:641
  70.3 1.2 %copy.10 = f32[128]{0:T(128)} copy(f32[128]{0:T(128)} %bitcast.3) | data formatting | bytes 1024

commit v3 on v2

--- a/solution.py
+++ b/solution.py
@@ -12,7 +12,7 @@
 F32 = jnp.float32
 LOG2E = 1.4426950408889634
 NEG = -1e30
-WROWS = 288
+WROWS = (320, 256)
 KROWS = 144
 
 
@@ -30,7 +30,7 @@
 
 def kernel(
     hid_hbm, q_hbm, gain_hbm, w_hbm, hw_hbm, fold_hbm, route_hbm, seg_hbm, out_ref,
-    gain_ref, hw_ref, fold_ref, route_ref, seg_ref, hw_row, hid, qv, wv, wpair, x3, wg, qout, qin, qx, kvout, kvin, win, kext, bias, onehot, onehot_t,
+    gain_ref, hw_ref, fold_ref, route_ref, seg_ref, hw_row, hid, qv, wv, wpair0, wpair1, x3, wg0, wg1, qout, qin, qx, kvout, kvin, win, kext, bias, onehot, onehot_t,
     kacc, vacc, high, acc, sbuf, ret_out, ret_in,
     load_sem, pair_send, pair_recv, xs_sem, xr_sem, qs_sem, qr_sem, ks_sem, kr_sem,
     rs_sem, rr_sem, ws_sem, wr_sem, gs_sem, gr_sem,
@@ -85,33 +85,34 @@
     wf_hi = wf.astype(BF).astype(F32)
     wf_lo = wf - wf_hi
     own_is_1 = core == 1
-    for g in range(2):
-        packs = []
-        for c in range(2):
+
+    def pick(a, b):
+        return jnp.where(own_is_1, b, a), jnp.where(own_is_1, a, b)
+
+    packs = []
+    for c in range(2):
+        rows = []
+        for g in range(2):
             at = 16 * c + 8 * g
-            rows = [wf_hi[at : at + 8], wf_lo[at : at + 8]]
-            pack = jnp.concatenate(rows, axis=0).astype(BF)
-            packs.append((wv[:, (2 * c + g) * 128 : (2 * c + g + 1) * 128], pack))
-        base = pl.multiple_of(core * WROWS, 32)
-        for n in range(2):
-            mine = jnp.where(own_is_1, packs[1][n], packs[0][n])
-            theirs = jnp.where(own_is_1, packs[0][n], packs[1][n])
-            if n == 0:
-                wg[g, chip, pl.ds(base, 256), :] = mine
-                wpair[g, 0:256, :] = theirs
-            else:
-                for side in range(2):
-                    lanes_of = slice(side * 128, (side + 1) * 128)
-                    at = 256 + 16 * side
-                    wg[g, chip, pl.ds(base + at, 16), :] = mine[:, lanes_of]
-                    wpair[g, at : at + 16, :] = theirs[:, lanes_of]
+            rows += [wf_hi[at : at + 8], wf_lo[at : at + 8]]
+        packs.append(jnp.concatenate(rows, axis=0).astype(BF))
+    mine, theirs = pick(packs[0], packs[1])
+    base = pl.multiple_of(core * WROWS[0], 32)
+    for side in range(2):
+        at = 256 + 32 * side
+        wg0[chip, pl.ds(base + at, 32), :] = mine[:, side * 128 : (side + 1) * 128]
+        wpair0[at : at + 32, :] = theirs[:, side * 128 : (side + 1) * 128]
+    for g, (wg, wpair) in enumerate(((wg0, wpair0), (wg1, wpair1))):
+        mine, theirs = pick(wv[:, g * 128 : g * 128 + 128], wv[:, g * 128 + 256 : g * 128 + 384])
+        wg[chip, pl.ds(pl.multiple_of(core * WROWS[g], 32), 256), :] = mine
+        wpair[0:256, :] = theirs
 
     pl.semaphore_wait(barrier, len(peers))
 
     def pair(g, side):
-        at = pl.ds(pl.multiple_of(side * WROWS, 32), WROWS)
+        at = pl.ds(pl.multiple_of(side * WROWS[g], 32), WROWS[g])
         return pltpu.make_async_remote_copy(
-            src_ref=wpair.at[g], dst_ref=wg.at[g, chip, at],
+            src_ref=(wpair0, wpair1)[g], dst_ref=(wg0, wg1)[g].at[chip, at],
             send_sem=pair_send.at[g], recv_sem=pair_recv.at[g],
             device_id=(d, 2 * chip + 1 - core), device_id_type=MESH,
         )
@@ -121,7 +122,7 @@
 
     class Gather:
         def __init__(self, g):
-            self.g, self.half, self.cut = g, WROWS, WROWS // 2
+            self.g, self.half, self.cut = g, WROWS[g], WROWS[g] // 2
 
         def part(self, par, kind):
             if kind < 2:
@@ -143,7 +144,7 @@
                 du = (0, -1, 1, 2)[group - 1]
                 at = near(par, du, back)
                 to = near(par, 0, step)
-            ref = wg.at[self.g, at, self.part(par, kind)]
+            ref = (wg0, wg1)[self.g].at[at, self.part(par, kind)]
             return pltpu.make_async_remote_copy(
                 src_ref=ref, dst_ref=ref,
                 send_sem=ws_sem.at[self.g, par, group, kind],
@@ -422,36 +423,39 @@
         return 0
 
     lax.fori_loop(0, 16, segment_keys, 0)
+    kext[16] = jnp.where(iota((256, 128), 1) < 8, NEG, 0.0).astype(BF)
 
     x_in.wait_recv()
     kacc[...] = jnp.zeros_like(kacc)
     vacc[...] = jnp.zeros_like(vacc)
 
-    def project(g, par, du, dv):
-        c = near(par, du, dv)
-        x = x3[2 * c + par]
-        base = pl.multiple_of(par * WROWS, 32)
-        kacc[g] += nn(x, wg[g, c, pl.ds(base, 256), :])
-        vacc[g] += nt(wg[g, c, pl.ds(base + 256, 16), :], x[:, 0:128]) + nt(
-            wg[g, c, pl.ds(base + 272, 16), :], x[:, 128:256]
-        )
-
-    def project_all(g, places):
+    def project(g, places):
+        wg = (wg0, wg1)[g]
+        k_sum = kacc[g]
+        v_sum = vacc[:, 0:32]
         for du, dv in places:
-            def body(par, _, du=du, dv=dv):
-                project(g, par, du, dv)
-                return 0
-
-            lax.fori_loop(0, 2, body, 0)
+            for par in range(2):
+                c = near(par, du, dv)
+                x = x3[2 * c + par]
+                base = par * WROWS[g]
+                k_sum += nn(x, wg[c, base : base + 256, :])
+                if g == 0:
+                    folded = jnp.concatenate(
+                        [wg[c, base + 256 : base + 288, :], wg[c, base + 288 : base + 320, :]], axis=1
+                    )
+                    v_sum += nt(x, folded)
+        kacc[g] = k_sum
+        if g == 0:
+            vacc[:, 0:32] = v_sum
 
     def project_rest(g):
         for group, place_of in ((1, (0, 2)), (2, (-1, 2)), (3, (1, 2)), (4, (2, 2))):
             weights[g].step6(group)
-            project_all(g, [place_of])
+            project(g, [place_of])
 
     def send_keys(g):
         k_rows = kacc[g].astype(BF)
-        v = vacc[g]
+        v = vacc[...].T[16 * g : 16 * g + 16]
         vf = v[0:8] + v[8:16]
         vf_hi = vf.astype(BF).astype(F32)
         v_rows = jnp.concatenate([vf_hi, vf - vf_hi, jnp.zeros((112, 256), F32)], axis=0)
@@ -491,16 +495,19 @@
             device_id=((d + dd) % 4, f), device_id_type=MESH,
         )
 
-    project_all(0, [(0, 0), (-1, 0), (1, 0), (0, -1), (0, 1), (2, 0)])
+    project(0, [(0, 0), (-1, 0), (1, 0)])
     weights[1].step2()
     weights[0].step5()
     weights[1].step3()
-    project_all(0, [(-1, -1), (-1, 1), (1, -1), (1, 1), (2, -1), (2, 1)])
+    project(0, [(0, -1), (0, 1), (2, 0)])
     weights[1].step4()
+    project(0, [(-1, -1), (-1, 1), (1, -1)])
+    project(0, [(1, 1), (2, -1), (2, 1)])
     project_rest(0)
     send_keys(0)
     weights[1].step5()
-    project_all(1, [(0, 0), (-1, 0), (1, 0), (0, -1), (0, 1), (2, 0)])
+    project(1, [(0, 0), (-1, 0), (1, 0)])
+    project(1, [(0, -1), (0, 1), (2, 0)])
 
     for dd, c in q_pairs:
         q_arrival(dd, c).wait_recv()
@@ -522,15 +529,19 @@
         qx[h, 0:128, :] = qh.astype(F32).T.astype(BF)
         qx[h, 128:256, :] = qseg
 
-    project_all(1, [(-1, -1), (-1, 1), (1, -1), (1, 1), (2, -1), (2, 1)])
+    project(1, [(-1, -1), (-1, 1), (1, -1)])
+    project(1, [(1, 1), (2, -1), (2, 1)])
     scale = LOG2E * 128.0 ** -0.5
-    ones = jnp.ones((16, 256), BF)
-
-    def attend(g, c, first):
+
+    def attend(g, chunks, first):
+        n = 256 * len(chunks)
+
         def scores(j):
-            key = jnp.concatenate([win[g, c, 0:256, :], kext[c]], axis=1)
+            key = jnp.concatenate(
+                [jnp.concatenate([win[g, c, 0:256, :], kext[e]], axis=1) for c, e in chunks], axis=0
+            )
             s = nn(key, qx[g * 8 + j])
-            sbuf[j] = s + bias[...] if first else s
+            sbuf[j, 0:n, :] = s + bias[...] if first else s
 
         for j in range(4):
             scores(j)
@@ -540,9 +551,9 @@
                     scores(j)
             for j in range(batch, batch + 4):
                 h = g * 8 + j
-                values = jnp.concatenate([win[g, c, 256:272, :], win[g, c, 272:288, :]], axis=1)
-                val = jnp.concatenate([values, ones], axis=0)
-                s = sbuf[j]
+                values = [win[g, c, at : at + 16, :] for c, e in chunks for at in (256, 272)]
+                val = jnp.concatenate([jnp.concatenate(values, axis=1), jnp.ones((16, n), BF)], axis=0)
+                s = sbuf[j, 0:n, :]
                 new = jnp.max(s, axis=0, keepdims=True)
                 if not first:
                     old = high[h]
@@ -552,34 +563,43 @@
                 acc[h] = part if first else acc[h] * jnp.exp2((old - new) * scale) + part
                 high[h] = new
 
-    def attend_row(g, row):
-        keys[g].row(row)
-
-        def body(k, _):
-            source = (y + k) % 4
-            c = chip - y - 4 * row + source
-            seen = (z >= row) & (c < chip) & (c >= chip - 8)
-
-            @pl.when(seen)
-            def _():
-                attend(g, c, False)
-
+    def attend_pairs(g, ok, place):
+        def body(i, _):
+            attend(g, [place(2 * i), place(2 * i + 1)], False)
             return 0
 
-        lax.fori_loop(0, 4, body, 0)
+        @pl.when(ok)
+        def _():
+            lax.fori_loop(0, 2, body, 0)
+
+    def attend_middle(g):
+        keys[g].row(1)
+        first = chip - y - 4
+        attend_pairs(g, z >= 1, lambda i: (first + i, first + i))
+
+    def attend_ends(g):
+        keys[g].row(0)
+        keys[g].row(2)
+
+        def place(i):
+            later = (i + 4 - y) // 4
+            seen = 1 - later * (1 - z // 2)
+            c = chip - y + i - 8 * later
+            return seen * c + (1 - seen) * chip, seen * c + (1 - seen) * 16
+
+        attend_pairs(g, (z >= 2) | (y >= 1), place)
 
     project_rest(1)
     send_keys(1)
     keys[0].forward()
-    attend(0, chip, True)
+    attend(0, [(chip, chip)], True)
     take_keys(1)
-    attend_row(0, 0)
+    attend_middle(0)
     keys[1].forward()
-    attend_row(0, 1)
-    attend_row(0, 2)
-    attend(1, chip, True)
-    for row in range(3):
-        attend_row(1, row)
+    attend_ends(0)
+    attend(1, [(chip, chip)], True)
+    attend_middle(1)
+    attend_ends(1)
 
     branch = jnp.zeros((1, 256), F32)
     for h in range(16):
@@ -653,24 +673,26 @@
             pltpu.VMEM((128, 8192), BF),
             pltpu.VMEM((128, 4096), BF),
             pltpu.VMEM((256, 1024), BF),
-            pltpu.VMEM((2, WROWS, 128), BF),
+            pltpu.VMEM((WROWS[0], 128), BF),
+            pltpu.VMEM((WROWS[1], 128), BF),
             pltpu.VMEM((32, 256, 256), BF),
-            pltpu.VMEM((2, 16, 2 * WROWS, 128), BF),
+            pltpu.VMEM((16, 2 * WROWS[0], 128), BF),
+            pltpu.VMEM((16, 2 * WROWS[1], 128), BF),
             pltpu.VMEM((4, 2, 32, 2176), BF),
             pltpu.VMEM((4, 2, 32, 2176), BF),
             pltpu.VMEM((16, 256, 256), BF),
             pltpu.VMEM((2, 4, 2, 32, 256), BF),
             pltpu.VMEM((2, 4, 2, 32, 256), BF),
             pltpu.VMEM((2, 16, 2 * KROWS, 128), BF),
-            pltpu.VMEM((16, 256, 128), BF),
+            pltpu.VMEM((17, 256, 128), BF),
             pltpu.VMEM((256, 256), F32),
             pltpu.VMEM((256, 256), BF),
             pltpu.VMEM((256, 256), BF),
             pltpu.VMEM((2, 256, 128), F32),
-            pltpu.VMEM((2, 16, 256), F32),
+            pltpu.VMEM((256, 128), F32),
             pltpu.VMEM((16, 1, 256), F32),
             pltpu.VMEM((16, 32, 256), F32),
-            pltpu.VMEM((8, 256, 256), F32),
+            pltpu.VMEM((8, 512, 256), F32),
             pltpu.VMEM((8, 256), F32),
             pltpu.VMEM((4, 2, 8, 256), F32),
             dma((8,)),

time: 71.6 us -> 66.6 us (0.930)
  Pallas kernels: 70.3 us -> 65.3 us
    pallas_call x1, Pallas kernels: 70.3 us -> 65.3 us  [on_device(): pl.pallas_call(kernel, out_shape=jax.ShapeDtypeStruct((1, 128), F32), in_...]
where the time goes in v3:
time: 66.6 us; the launch traced here: 66.5 us
  Pallas kernels  65.3 us (98%)
  local copies, waits for them, and re-layouts  1.19 us (2%)
    pallas_call x1, Pallas kernels, on_device(): pl.pallas_call(kernel, out_shape=jax.ShapeDtypeStruct((1, 128), F32), in_...  65.3 us

profile of v3, /device:TPU:65, one launch (start us, length us, event | category | flops | bytes accessed | tf_op | source)
XLA Modules:
  0.0 66.5 jit_solution(742762149226009444)
XLA Ops:
  0.0 65.3 %shard_map.82 = f32[1,128]{1,0:T(1,128)} custom-call(bf16[128,8192]{1,0:T(8,128)(2,1)} %hid_hbm.1, bf16[128,4096]{1,0:T(8,128)(2,1)} %q_hbm.1, f32[1,8192]{1,0:T(1,128)} %bitcast.2, bf16[256,1024]{1,0:T(8,128)(2,1)} %w_hbm.1, bf16[8192]{0:T(1024)(128)(2,1)} %hw_hbm.1, bf16[4096]{0:T(1024)(128)(2,1)} %fold_hbm.1, s32[2,128]{1,0:T(2,128)} %route_hbm.1, ...), custom_call_target="tpu_custom_call" | custom-call | flops 10000000000 | bytes 4000000 | tf_op jit(solution)/shard_map/pallas_call | solution.py:661
  65.3 1.2 %copy.10 = f32[128]{0:T(128)} copy(f32[128]{0:T(128)} %bitcast.3) | data formatting | bytes 1024

commit v4 on v3

--- a/solution.py
+++ b/solution.py
@@ -12,8 +12,8 @@
 F32 = jnp.float32
 LOG2E = 1.4426950408889634
 NEG = -1e30
-WROWS = (320, 256)
-KROWS = 144
+WROWS = (288, 256)
+KPART = ((0, 144), (144, 128))
 
 
 def nn(a, b):
@@ -82,26 +82,18 @@
     fold_t = jnp.concatenate([head_row] * 4, axis=1)
     fold_t = jnp.where(iota((32, 512), 0) // 8 == iota((32, 512), 1) // 128, fold_t, 0.0).astype(BF)
     wf = nt(fold_t, wv[:, 512:1024])
-    wf_hi = wf.astype(BF).astype(F32)
-    wf_lo = wf - wf_hi
     own_is_1 = core == 1
 
     def pick(a, b):
         return jnp.where(own_is_1, b, a), jnp.where(own_is_1, a, b)
 
-    packs = []
-    for c in range(2):
-        rows = []
-        for g in range(2):
-            at = 16 * c + 8 * g
-            rows += [wf_hi[at : at + 8], wf_lo[at : at + 8]]
-        packs.append(jnp.concatenate(rows, axis=0).astype(BF))
+    packs = [wf[16 * c : 16 * c + 16].astype(BF) for c in range(2)]
     mine, theirs = pick(packs[0], packs[1])
     base = pl.multiple_of(core * WROWS[0], 32)
     for side in range(2):
-        at = 256 + 32 * side
-        wg0[chip, pl.ds(base + at, 32), :] = mine[:, side * 128 : (side + 1) * 128]
-        wpair0[at : at + 32, :] = theirs[:, side * 128 : (side + 1) * 128]
+        at = 256 + 16 * side
+        wg0[chip, pl.ds(base + at, 16), :] = mine[:, side * 128 : (side + 1) * 128]
+        wpair0[at : at + 16, :] = theirs[:, side * 128 : (side + 1) * 128]
     for g, (wg, wpair) in enumerate(((wg0, wpair0), (wg1, wpair1))):
         mine, theirs = pick(wv[:, g * 128 : g * 128 + 128], wv[:, g * 128 + 256 : g * 128 + 384])
         wg[chip, pl.ds(pl.multiple_of(core * WROWS[g], 32), 256), :] = mine
@@ -212,7 +204,7 @@
             self.g = g
 
         def copy(self, n, at, par, to):
-            ref = win.at[self.g, at, pl.ds(par * KROWS, KROWS)]
+            ref = win.at[self.g, at, pl.ds(*KPART[par])]
             return pltpu.make_async_remote_copy(
                 src_ref=ref, dst_ref=ref,
                 send_sem=gs_sem.at[self.g, n], recv_sem=gr_sem.at[self.g, n],
@@ -389,6 +381,8 @@
     total, dot = lax.fori_loop(0, 32, squares, (zero, zero))
     root = lax.rsqrt(jnp.sum(total, axis=1, keepdims=True) * (1.0 / 8192.0) + 1e-05)
     residual = jnp.sum(dot, axis=1, keepdims=True)
+    weights[0].step2()
+    weights[1].step1()
     my_rows = pl.ds(pl.multiple_of(core * 128, 128), 128)
 
     def normalise(i, _):
@@ -409,9 +403,8 @@
         device_id=(d, 2 * chip + 1 - core), device_id_type=MESH,
     )
     x_copy.start()
-    weights[0].step2()
-    weights[1].step1()
     weights[0].step3()
+    weights[1].step2()
     weights[0].step4()
 
     def segment_keys(i, _):
@@ -432,7 +425,7 @@
     def project(g, places):
         wg = (wg0, wg1)[g]
         k_sum = kacc[g]
-        v_sum = vacc[:, 0:32]
+        v_sum = vacc[:, 0:16]
         for du, dv in places:
             for par in range(2):
                 c = near(par, du, dv)
@@ -441,12 +434,12 @@
                 k_sum += nn(x, wg[c, base : base + 256, :])
                 if g == 0:
                     folded = jnp.concatenate(
-                        [wg[c, base + 256 : base + 288, :], wg[c, base + 288 : base + 320, :]], axis=1
+                        [wg[c, base + 256 : base + 272, :], wg[c, base + 272 : base + 288, :]], axis=1
                     )
                     v_sum += nt(x, folded)
         kacc[g] = k_sum
         if g == 0:
-            vacc[:, 0:32] = v_sum
+            vacc[:, 0:16] = v_sum
 
     def project_rest(g):
         for group, place_of in ((1, (0, 2)), (2, (-1, 2)), (3, (1, 2)), (4, (2, 2))):
@@ -455,10 +448,8 @@
 
     def send_keys(g):
         k_rows = kacc[g].astype(BF)
-        v = vacc[...].T[16 * g : 16 * g + 16]
-        vf = v[0:8] + v[8:16]
-        vf_hi = vf.astype(BF).astype(F32)
-        v_rows = jnp.concatenate([vf_hi, vf - vf_hi, jnp.zeros((112, 256), F32)], axis=0)
+        vf = vacc[...].T[8 * g : 8 * g + 8]
+        v_rows = jnp.concatenate([vf, jnp.zeros((120, 256), F32)], axis=0)
         v_cols = v_rows.T.astype(BF)
         for s in range(2):
             for b in range(4):
@@ -474,10 +465,9 @@
             k_arrival(g, dd).wait_recv()
         got_k = kvin[g, :, :, :, 0:128].reshape(256, 128)
         got_v = kvin[g, :, :, :, 128:256].reshape(256, 128).astype(F32).T[0:16].astype(BF)
-        values = nn(got_v, onehot[...]).astype(BF)
+        values = nn(got_v, onehot[...])[0:8]
         win[g, chip, 0:256, :] = nn(onehot_t[...], got_k).astype(BF)
-        win[g, chip, 256:272, :] = values[:, 0:128]
-        win[g, chip, 272:288, :] = values[:, 128:256]
+        win[g, chip, 256:272, :] = jnp.concatenate([values[:, 0:128], values[:, 128:256]], axis=0).astype(BF)
         keys[g].begin()
 
     def k_copy(g, dd):
@@ -496,7 +486,6 @@
         )
 
     project(0, [(0, 0), (-1, 0), (1, 0)])
-    weights[1].step2()
     weights[0].step5()
     weights[1].step3()
     project(0, [(0, -1), (0, 1), (2, 0)])
@@ -535,6 +524,9 @@
 
     def attend(g, chunks, first):
         n = 256 * len(chunks)
+        values = [win[g, c, 256:272, :].astype(F32) for c, e in chunks]
+        values = jnp.concatenate([v[at : at + 8] for v in values for at in (0, 8)], axis=1)
+        val = jnp.concatenate([values, jnp.ones((8, n), F32)], axis=0).astype(BF)
 
         def scores(j):
             key = jnp.concatenate(
@@ -551,8 +543,6 @@
                     scores(j)
             for j in range(batch, batch + 4):
                 h = g * 8 + j
-                values = [win[g, c, at : at + 16, :] for c, e in chunks for at in (256, 272)]
-                val = jnp.concatenate([jnp.concatenate(values, axis=1), jnp.ones((16, n), BF)], axis=0)
                 s = sbuf[j, 0:n, :]
                 new = jnp.max(s, axis=0, keepdims=True)
                 if not first:
@@ -605,7 +595,7 @@
     for h in range(16):
         a = acc[h]
         j = h % 8
-        branch = branch + (a[j : j + 1] + a[8 + j : 9 + j]) / a[16:17]
+        branch = branch + a[j : j + 1] / a[8:9]
     ret_out[...] = jnp.broadcast_to(branch, (8, 256))
 
     def r_copy(dd, c):
@@ -683,7 +673,7 @@
             pltpu.VMEM((16, 256, 256), BF),
             pltpu.VMEM((2, 4, 2, 32, 256), BF),
             pltpu.VMEM((2, 4, 2, 32, 256), BF),
-            pltpu.VMEM((2, 16, 2 * KROWS, 128), BF),
+            pltpu.VMEM((2, 16, 272, 128), BF),
             pltpu.VMEM((17, 256, 128), BF),
             pltpu.VMEM((256, 256), F32),
             pltpu.VMEM((256, 256), BF),
@@ -691,7 +681,7 @@
             pltpu.VMEM((2, 256, 128), F32),
             pltpu.VMEM((256, 128), F32),
             pltpu.VMEM((16, 1, 256), F32),
-            pltpu.VMEM((16, 32, 256), F32),
+            pltpu.VMEM((16, 16, 256), F32),
             pltpu.VMEM((8, 512, 256), F32),
             pltpu.VMEM((8, 256), F32),
             pltpu.VMEM((4, 2, 8, 256), F32),

time: 66.6 us -> 63.1 us (0.947)
  Pallas kernels: 65.3 us -> 61.8 us
    pallas_call x1, Pallas kernels: 65.3 us -> 61.8 us  [on_device(): pl.pallas_call(kernel, out_shape=jax.ShapeDtypeStruct((1, 128), F32), in_...]
where the time goes in v4:
time: 63.1 us; the launch traced here: 63 us
  Pallas kernels  61.8 us (98%)
  local copies, waits for them, and re-layouts  1.19 us (2%)
    pallas_call x1, Pallas kernels, on_device(): pl.pallas_call(kernel, out_shape=jax.ShapeDtypeStruct((1, 128), F32), in_...  61.8 us

profile of v4, /device:TPU:65, one launch (start us, length us, event | category | flops | bytes accessed | tf_op | source)
XLA Modules:
  0.0 63.0 jit_solution(14018869424497770604)
XLA Ops:
  0.0 61.8 %shard_map.82 = f32[1,128]{1,0:T(1,128)} custom-call(bf16[128,8192]{1,0:T(8,128)(2,1)} %hid_hbm.1, bf16[128,4096]{1,0:T(8,128)(2,1)} %q_hbm.1, f32[1,8192]{1,0:T(1,128)} %bitcast.2, bf16[256,1024]{1,0:T(8,128)(2,1)} %w_hbm.1, bf16[8192]{0:T(1024)(128)(2,1)} %hw_hbm.1, bf16[4096]{0:T(1024)(128)(2,1)} %fold_hbm.1, s32[2,128]{1,0:T(2,128)} %route_hbm.1, ...), custom_call_target="tpu_custom_call" | custom-call | flops 10000000000 | bytes 4000000 | tf_op jit(solution)/shard_map/pallas_call | solution.py:651
  61.8 1.2 %copy.10 = f32[128]{0:T(128)} copy(f32[128]{0:T(128)} %bitcast.3) | data formatting | bytes 1024

commit v5 on v4

--- a/solution.py
+++ b/solution.py
@@ -13,7 +13,7 @@
 LOG2E = 1.4426950408889634
 NEG = -1e30
 WROWS = (288, 256)
-KPART = ((0, 144), (144, 128))
+KPART = ((0, 96), (96, 176))
 
 
 def nn(a, b):
@@ -255,12 +255,12 @@
         def begin(self):
             for e in (1, 3, 2):
                 self.send(self.first_y, e)
-            for j in (1, 2):
-                self.send(self.first_z, j)
-            for j in (1, 2):
-                self.send(self.then_z, 0, j)
+            self.send(self.first_z, 1)
+            self.send(self.then_z, 0, 1)
             for e in (1, 3, 2):
                 self.send(self.then_y, e, 0)
+            self.send(self.first_z, 2)
+            self.send(self.then_z, 0, 2)
 
         def forward(self):
             self.wait(self.first_z, 1)
@@ -268,8 +268,9 @@
                 self.send(self.then_y, e, 1)
             for e in (1, 3, 2):
                 self.wait(self.first_y, e)
-                for j in (1, 2):
-                    self.send(self.then_z, (4 - e) % 4, j)
+                self.send(self.then_z, 4 - e, 1)
+            for e in (1, 3, 2):
+                self.send(self.then_z, 4 - e, 2)
             self.wait(self.first_z, 2)
             for e in (1, 3, 2):
                 self.send(self.then_y, e, 2)

time: 63.1 us -> 60.9 us (0.965)
  Pallas kernels: 61.8 us -> 59.5 us
    pallas_call x1, Pallas kernels: 61.8 us -> 59.5 us  [on_device(): pl.pallas_call(kernel, out_shape=jax.ShapeDtypeStruct((1, 128), F32), in_...]
where the time goes in v5:
time: 60.9 us; the launch traced here: 60.7 us
  Pallas kernels  59.5 us (98%)
  local copies, waits for them, and re-layouts  1.19 us (2%)
    pallas_call x1, Pallas kernels, on_device(): pl.pallas_call(kernel, out_shape=jax.ShapeDtypeStruct((1, 128), F32), in_...  59.5 us

profile of v5, /device:TPU:65, one launch (start us, length us, event | category | flops | bytes accessed | tf_op | source)
XLA Modules:
  0.0 60.7 jit_solution(4868710599294777061)
XLA Ops:
  0.0 59.5 %shard_map.82 = f32[1,128]{1,0:T(1,128)} custom-call(bf16[128,8192]{1,0:T(8,128)(2,1)} %hid_hbm.1, bf16[128,4096]{1,0:T(8,128)(2,1)} %q_hbm.1, f32[1,8192]{1,0:T(1,128)} %bitcast.2, bf16[256,1024]{1,0:T(8,128)(2,1)} %w_hbm.1, bf16[8192]{0:T(1024)(128)(2,1)} %hw_hbm.1, bf16[4096]{0:T(1024)(128)(2,1)} %fold_hbm.1, s32[2,128]{1,0:T(2,128)} %route_hbm.1, ...), custom_call_target="tpu_custom_call" | custom-call | flops 10000000000 | bytes 4000000 | tf_op jit(solution)/shard_map/pallas_call | solution.py:652
  59.6 1.2 %copy.10 = f32[128]{0:T(128)} copy(f32[128]{0:T(128)} %bitcast.3) | data formatting | bytes 1024

commit v6 on v5

--- a/solution.py
+++ b/solution.py
@@ -30,11 +30,12 @@
 
 def kernel(
     hid_hbm, q_hbm, gain_hbm, w_hbm, hw_hbm, fold_hbm, route_hbm, seg_hbm, out_ref,
-    gain_ref, hw_ref, fold_ref, route_ref, seg_ref, hw_row, hid, qv, wv, wpair0, wpair1, x3, wg0, wg1, qout, qin, qx, kvout, kvin, win, kext, bias, onehot, onehot_t,
+    gain_ref, hw_ref, fold_ref, route_ref, seg_ref, hw_row, hid, qv, wv, wpair0, wpair1, x3, wg0, wg1, qout, qin, qx, kvout0, kvout1, kvin0, kvin1, win, kext, bias, onehot, onehot_t,
     kacc, vacc, high, acc, sbuf, ret_out, ret_in,
     load_sem, pair_send, pair_recv, xs_sem, xr_sem, qs_sem, qr_sem, ks_sem, kr_sem,
     rs_sem, rr_sem, ws_sem, wr_sem, gs_sem, gr_sem,
 ):
+    kvout, kvin = (kvout0, kvout1), (kvin0, kvin1)
     d = lax.axis_index("dp")
     f = lax.axis_index("fsdp")
     chip = f // 2
@@ -337,7 +338,7 @@
                 qout[b, c, :, dst] = block[b * 32 : (b + 1) * 32]
         return 0
 
-    lax.fori_loop(0, 8, sort_q, 0)
+    lax.fori_loop(0, 8, sort_q, 0, unroll=4)
 
     def q_copy(dd, c):
         b = (d + dd) % 4
@@ -379,7 +380,7 @@
         return total + x * x, dot + x * hw_row[:, at]
 
     zero = jnp.zeros((128, 256), F32)
-    total, dot = lax.fori_loop(0, 32, squares, (zero, zero))
+    total, dot = lax.fori_loop(0, 32, squares, (zero, zero), unroll=4)
     root = lax.rsqrt(jnp.sum(total, axis=1, keepdims=True) * (1.0 / 8192.0) + 1e-05)
     residual = jnp.sum(dot, axis=1, keepdims=True)
     weights[0].step2()
@@ -392,7 +393,7 @@
         x3[i, my_rows, :] = nn(perm, normed).astype(BF)
         return 0
 
-    lax.fori_loop(0, 32, normalise, 0)
+    lax.fori_loop(0, 32, normalise, 0, unroll=4)
     x_rows = x3.at[:, my_rows, :]
     x_copy = pltpu.make_async_remote_copy(
         src_ref=x_rows, dst_ref=x_rows, send_sem=xs_sem, recv_sem=xr_sem,
@@ -416,7 +417,7 @@
         kext[i] = part.T.astype(BF)
         return 0
 
-    lax.fori_loop(0, 16, segment_keys, 0)
+    lax.fori_loop(0, 16, segment_keys, 0, unroll=4)
     kext[16] = jnp.where(iota((256, 128), 1) < 8, NEG, 0.0).astype(BF)
 
     x_in.wait_recv()
@@ -449,39 +450,44 @@
 
     def send_keys(g):
         k_rows = kacc[g].astype(BF)
-        vf = vacc[...].T[8 * g : 8 * g + 8]
-        v_rows = jnp.concatenate([vf, jnp.zeros((120, 256), F32)], axis=0)
-        v_cols = v_rows.T.astype(BF)
+        if g == 0:
+            v_cols = vacc[...].astype(BF)
         for s in range(2):
             for b in range(4):
                 at = s * 128 + b * 32
-                kvout[g, b, s, :, 0:128] = k_rows[at : at + 32]
-                kvout[g, b, s, :, 128:256] = v_cols[at : at + 32]
+                kvout[g][b, s, :, 0:128] = k_rows[at : at + 32]
+                if g == 0:
+                    kvout[0][b, s, :, 128:256] = v_cols[at : at + 32]
         for dd in range(1, 4):
             k_copy(g, dd).start()
-        kvin[g, d] = kvout[g, d]
+        kvin[g][d] = kvout[g][d]
 
     def take_keys(g):
         for dd in range(1, 4):
             k_arrival(g, dd).wait_recv()
-        got_k = kvin[g, :, :, :, 0:128].reshape(256, 128)
-        got_v = kvin[g, :, :, :, 128:256].reshape(256, 128).astype(F32).T[0:16].astype(BF)
-        values = nn(got_v, onehot[...])[0:8]
+        got_k = kvin[g][:, :, :, 0:128].reshape(256, 128)
         win[g, chip, 0:256, :] = nn(onehot_t[...], got_k).astype(BF)
-        win[g, chip, 256:272, :] = jnp.concatenate([values[:, 0:128], values[:, 128:256]], axis=0).astype(BF)
+        if g == 0:
+            got_v = kvin[0][:, :, :, 128:256].reshape(256, 128).astype(F32).T[0:16].astype(BF)
+            values = nn(got_v, onehot[...])
+            for n in range(2):
+                of_head = values[8 * n : 8 * n + 8]
+                win[n, chip, 256:272, :] = jnp.concatenate(
+                    [of_head[:, 0:128], of_head[:, 128:256]], axis=0
+                ).astype(BF)
         keys[g].begin()
 
     def k_copy(g, dd):
         b = (d + dd) % 4
         return pltpu.make_async_remote_copy(
-            src_ref=kvout.at[g, b], dst_ref=kvin.at[g, d],
+            src_ref=kvout[g].at[b], dst_ref=kvin[g].at[d],
             send_sem=ks_sem.at[g, dd], recv_sem=kr_sem.at[g, dd],
             device_id=(b, f), device_id_type=MESH,
         )
 
     def k_arrival(g, dd):
         return pltpu.make_async_remote_copy(
-            src_ref=kvout.at[g, d], dst_ref=kvin.at[g, (d - dd + 4) % 4],
+            src_ref=kvout[g].at[d], dst_ref=kvin[g].at[(d - dd + 4) % 4],
             send_sem=ks_sem.at[g, dd], recv_sem=kr_sem.at[g, dd],
             device_id=((d + dd) % 4, f), device_id_type=MESH,
         )
@@ -618,8 +624,20 @@
     for dd, c in q_pairs:
         r_copy(dd, c).start()
     ret_in[d, core] = ret_out[...]
+    x_copy.wait_send()
+    for g in range(2):
+        pair(g, core).wait_send()
+        weights[g].finish()
+        keys[g].finish()
+    for dd, c in q_pairs:
+        q_copy(dd, c).wait_send()
+    for g in range(2):
+        for dd in range(1, 4):
+            k_copy(g, dd).wait_send()
     for dd, c in q_pairs:
         r_arrival(dd, c).wait_recv()
+    for dd, c in q_pairs:
+        r_copy(dd, c).wait_send()
 
     lane = (d * 64 + core * 32).astype(F32) + rank_col
     lanes = iota((128, 256), 1).astype(F32)
@@ -629,18 +647,6 @@
         value = value + jnp.where((lanes == lane) & (bin_col == float(b)), row, 0.0)
     score = jnp.sum(value, axis=1, keepdims=True) + residual
     out_ref[...] = jnp.sum(jnp.where(eye, score, 0.0), axis=0, keepdims=True)
-
-    x_copy.wait_send()
-    for g in range(2):
-        pair(g, core).wait_send()
-        weights[g].finish()
-        keys[g].finish()
-    for dd, c in q_pairs:
-        q_copy(dd, c).wait_send()
-        r_copy(dd, c).wait_send()
-    for g in range(2):
-        for dd in range(1, 4):
-            k_copy(g, dd).wait_send()
 
 
 def on_device(
@@ -672,8 +678,10 @@
             pltpu.VMEM((4, 2, 32, 2176), BF),
             pltpu.VMEM((4, 2, 32, 2176), BF),
             pltpu.VMEM((16, 256, 256), BF),
-            pltpu.VMEM((2, 4, 2, 32, 256), BF),
-            pltpu.VMEM((2, 4, 2, 32, 256), BF),
+            pltpu.VMEM((4, 2, 32, 256), BF),
+            pltpu.VMEM((4, 2, 32, 128), BF),
+            pltpu.VMEM((4, 2, 32, 256), BF),
+            pltpu.VMEM((4, 2, 32, 128), BF),
             pltpu.VMEM((2, 16, 272, 128), BF),
             pltpu.VMEM((17, 256, 128), BF),
             pltpu.VMEM((256, 256), F32),

time: 60.9 us -> 60.4 us (level)
  no operation moved by 1% of the time
where the time goes in v6:
time: 60.4 us; the launch traced here: 60.3 us
  Pallas kernels  59.1 us (98%)
  local copies, waits for them, and re-layouts  1.19 us (2%)
    pallas_call x1, Pallas kernels, on_device(): pl.pallas_call(kernel, out_shape=jax.ShapeDtypeStruct((1, 128), F32), in_...  59.1 us

profile of v6, /device:TPU:65, one launch (start us, length us, event | category | flops | bytes accessed | tf_op | source)
XLA Modules:
  0.0 60.3 jit_solution(10395469804005340895)
XLA Ops:
  0.0 59.1 %shard_map.82 = f32[1,128]{1,0:T(1,128)} custom-call(bf16[128,8192]{1,0:T(8,128)(2,1)} %hid_hbm.1, bf16[128,4096]{1,0:T(8,128)(2,1)} %q_hbm.1, f32[1,8192]{1,0:T(1,128)} %bitcast.2, bf16[256,1024]{1,0:T(8,128)(2,1)} %w_hbm.1, bf16[8192]{0:T(1024)(128)(2,1)} %hw_hbm.1, bf16[4096]{0:T(1024)(128)(2,1)} %fold_hbm.1, s32[2,128]{1,0:T(2,128)} %route_hbm.1, ...), custom_call_target="tpu_custom_call" | custom-call | flops 10000000000 | bytes 4000000 | tf_op jit(solution)/shard_map/pallas_call | solution.py:658
  59.1 1.2 %copy.10 = f32[128]{0:T(128)} copy(f32[128]{0:T(128)} %bitcast.3) | data formatting | bytes 1024
